TPU v7x, 512 devices: a whole 4x8x8 slice. The times are simulated.
512 devices in a mesh: space: 32 (over x, y), bins: 16 (over z, core).
Axes of the slice: x: 4, y: 8, z: 8, core: 2. Of those that a mesh axis runs over, the one named last changes fastest.
Arguments:
- swell_density_ensemble: bfloat16 [768, 32, 8192], P('bins', None, 'space'), may hold values from 0.049804688 to 2
- neighbors: int32 [4, 8192], P(None, 'space'), may hold values from -1 to 8191, as said below
- obs_operator: float32 [16, 768], P(None, 'bins'), may hold values from -0.21875 to 0.21875
- obs_point: int32 [2048], P('space'), may hold values from 0 to 8191, as said below
- obs_type: int32 [2048], P('space'), may hold values from 0 to 15
- obs_value: float32 [2048], P('space'), may hold values from -8 to 8
- obs_var: float32 [2048], P('space'), may hold values from 0.05 to 0.5
- obs_list: int32 [32, 8192], P(None, 'space'), may hold values from -1 to 2047, as said below
- obs_count: int32 [8192], P('space'), may hold values from 0 to 32, as said below
Outputs:
- analysis: bfloat16 [768, 32, 8192], P('bins', None, 'space')
Inputs may be any that keep to these rules, and one draw needn't show every extreme that they name: `neighbors`: row k of point p holds p - 32, p + 32, p - 1 or p + 1 for k = 0, 1, 2, 3, the last two only within p's column, or -1 where that neighbour is land or off the grid. `obs_point`: observation j lies on a point of tile j // 64, where tile t holds points t * 256 to (t + 1) * 256 - 1. `obs_list`: for k < obs_count[p], slot k of point p names an observation whose point lies within 6 cells of p (squared column offset plus squared row offset at most 6^2), so in p's tile or a tile beside it; names in one list are distinct; other slots hold -1. `obs_count`: reaches 32 at some point of every tile.
All inputs are finite; a program needn't handle non-finite values.
Results may differ from a plain program's by a relative error of at most 0.0059.
Values may be sent and summed in bfloat16 or wider, within the bound.
A program may use at most 64 MiB of HBM per device.

v0:
```python
import jax
import jax.numpy as jnp
from jax import lax
from jax.sharding import PartitionSpec as P

ND = 24
ROWS = 32
LOC_R = 6
NS_ITERS = 8


courant_max = 0.7
freq_ratio = 1.1


def with_halo(cells, sides, width):
    for axis, dim in sides:
        count = lax.axis_size(axis)
        ends = count - 1
        head = lax.slice_in_dim(cells, 0, width, axis=dim)
        tail = lax.slice_in_dim(cells, cells.shape[dim] - width, cells.shape[dim], axis=dim)
        cells = jnp.concatenate(
            [
                lax.ppermute(tail, axis, [(i, (i + 1) % count) for i in range(ends)]),
                cells,
                lax.ppermute(head, axis, [((i + 1) % count, i) for i in range(ends)]),
            ],
            axis=dim,
        )
    return cells


def from_everyone(value, axis):
    count = lax.axis_size(axis)
    return lax.all_to_all(
        jnp.broadcast_to(value[None], (count, *value.shape)), axis, 0, 0, tiled=True
    )


def of_everyone(value, axis):
    return from_everyone(value, axis).sum(axis=0)


def joined_along(pieces, dim):
    dims = list(pieces.shape[1:])
    dims[dim] *= pieces.shape[0]
    return jnp.moveaxis(pieces, 0, dim).reshape(dims)


def gather_directly(value, axis, dim):
    return joined_along(from_everyone(value, axis), dim)


def courant(frequency_direction_number):
    direction = (frequency_direction_number % ND).astype(jnp.float32)
    band_index = (frequency_direction_number // ND).astype(jnp.float32)
    angle = 2.0 * jnp.pi * (direction + 0.5) / ND
    speed = courant_max * jnp.exp(-band_index * jnp.log(freq_ratio))
    cosine = jnp.cos(angle)
    sine_value = jnp.sin(angle)
    return (
        (speed * jnp.abs(cosine))[:, None, None],
        (speed * jnp.abs(sine_value))[:, None, None],
        (cosine > 0)[:, None, None],
        (sine_value > 0)[:, None, None],
    )


def donor_cell_propagate(padded_with_neighbours, outer_edge_inflow, frequency_direction_number):
    inner = padded_with_neighbours.shape[2] - 2 * ROWS
    swell_variance_density = padded_with_neighbours[:, :, ROWS : ROWS + inner].astype(jnp.float32)
    from_west = padded_with_neighbours[:, :, 0:inner].astype(jnp.float32) * outer_edge_inflow[0]
    from_east = (
        padded_with_neighbours[:, :, 2 * ROWS : 2 * ROWS + inner].astype(jnp.float32)
        * outer_edge_inflow[1]
    )
    from_south = (
        padded_with_neighbours[:, :, ROWS - 1 : ROWS - 1 + inner].astype(jnp.float32)
        * outer_edge_inflow[2]
    )
    from_north = (
        padded_with_neighbours[:, :, ROWS + 1 : ROWS + 1 + inner].astype(jnp.float32)
        * outer_edge_inflow[3]
    )
    courant_x, courant_y, east_ward, north_ward = courant(frequency_direction_number)
    inflow_x = jnp.where(east_ward, from_west, from_east)
    inflow_y = jnp.where(north_ward, from_south, from_north)
    return (
        swell_variance_density
        - courant_x * (swell_variance_density - inflow_x)
        - courant_y * (swell_variance_density - inflow_y)
    ).astype(jnp.bfloat16)


def obs_package(predicted, obs_point, obs_value, obs_var):
    ens_mean = jnp.mean(predicted, axis=0)
    weight = lax.rsqrt(obs_var)
    anomaly = (predicted - ens_mean[None]) * weight[None]
    innovation = (obs_value - ens_mean) * weight
    obs_col = (obs_point // ROWS).astype(jnp.float32)
    obs_row = (obs_point % ROWS).astype(jnp.float32)
    return jnp.concatenate([anomaly, innovation[None], obs_col[None], obs_row[None]], axis=0)


def analysis_weights(anomaly, innovation, taper):
    members = anomaly.shape[0]
    highest = lax.Precision.HIGHEST
    identity = jnp.eye(members, dtype=jnp.float32)[None]
    weighted = anomaly * taper[None]
    matrix = identity + jnp.einsum("ikn,jkn->nij", weighted, anomaly, precision=highest) / (
        members - 1.0
    )
    obs_pull = jnp.einsum("ikn,kn->ni", weighted, innovation, precision=highest) / (members - 1.0)
    scale = jnp.sqrt(jnp.sum(matrix * matrix, axis=(1, 2)))
    current = matrix / scale[:, None, None]
    inverse = jnp.broadcast_to(identity, matrix.shape)

    def newton_step(iteration, carried):
        current, inverse = carried
        factor = 1.5 * identity - 0.5 * jnp.einsum(
            "nij,njk->nik", inverse, current, precision=highest
        )
        current = jnp.einsum("nij,njk->nik", current, factor, precision=highest)
        inverse = jnp.einsum("nij,njk->nik", factor, inverse, precision=highest)
        return (current, inverse)

    current, inverse = lax.fori_loop(0, NS_ITERS, newton_step, (current, inverse))
    inv_root = inverse / jnp.sqrt(scale)[:, None, None]
    half_step = jnp.einsum("nij,nj->ni", inv_root, obs_pull, precision=highest)
    mean_shift = jnp.einsum("nij,nj->ni", inv_root, half_step, precision=highest)
    return jnp.transpose(inv_root + mean_shift[:, :, None], (1, 2, 0))


def point_weights(package, slot_ids, counts, first_point):
    members = package.shape[0] - 3
    safe_slots = jnp.maximum(slot_ids, 0)
    picked = jnp.take(package, safe_slots, axis=1)
    points = first_point + jnp.arange(slot_ids.shape[1], dtype=jnp.int32)
    point_col = (points // ROWS).astype(jnp.float32)
    point_row = (points % ROWS).astype(jnp.float32)
    active = (jnp.arange(slot_ids.shape[0], dtype=jnp.int32)[:, None] < counts[None]).astype(
        jnp.float32
    )
    distance = (picked[members + 1] - point_col[None]) ** 2 + (
        picked[members + 2] - point_row[None]
    ) ** 2
    taper = (1.0 - distance / (2.0 * LOC_R * LOC_R)) ** 2 * active
    return analysis_weights(picked[:members], picked[members], taper)


def combine_ensemble_coefficients(prior_ensemble_densities, ensemble_mixing_coefficients):
    swell_variance_density = prior_ensemble_densities.astype(jnp.float32)
    ens_mean = jnp.mean(swell_variance_density, axis=1, keepdims=True)
    anomaly = swell_variance_density - ens_mean
    moved = jnp.einsum(
        "bin,imn->bmn", anomaly, ensemble_mixing_coefficients, precision=lax.Precision.HIGHEST
    )
    return (ens_mean + moved).astype(jnp.bfloat16)


def per_device(
    swell_density_ensemble,
    neighbors,
    obs_operator,
    obs_point,
    obs_type,
    obs_value,
    obs_var,
    obs_list,
    obs_count,
):
    bins_local, members, local_points = swell_density_ensemble.shape
    present_patch_number = lax.axis_index("space")
    bin_group = lax.axis_index("bins")
    bin_devices = lax.axis_size("bins")
    padded_with_neighbours = with_halo(swell_density_ensemble, (("space", 2),), ROWS)
    frequency_direction_number = bin_group * bins_local + jnp.arange(bins_local, dtype=jnp.int32)
    outer_edge_inflow = (neighbors >= 0).astype(jnp.float32)
    prior_ensemble_densities = donor_cell_propagate(
        padded_with_neighbours, outer_edge_inflow, frequency_direction_number
    )
    first_point = present_patch_number * local_points
    measured_locations = obs_point - first_point
    lattice_width_count = jnp.take(prior_ensemble_densities, measured_locations, axis=2).astype(
        jnp.float32
    )
    type_onehot = (
        obs_type[:, None] == jnp.arange(obs_operator.shape[0], dtype=jnp.int32)[None]
    ).astype(jnp.float32)
    obs_rows = jnp.dot(type_onehot, obs_operator, precision=lax.Precision.HIGHEST)
    partial_value = jnp.einsum(
        "bmo,ob->mo", lattice_width_count, obs_rows, precision=lax.Precision.HIGHEST
    )
    predicted = of_everyone(partial_value, "bins")
    package = obs_package(predicted, obs_point, obs_value, obs_var)
    obs_wide = with_halo(package, (("space", 1),), package.shape[1])
    offset = (present_patch_number - 1) * package.shape[1]
    slot_ids = jnp.where(obs_list >= 0, obs_list - offset, -1)
    share_size = local_points // bin_devices
    own_slots = lax.dynamic_slice_in_dim(slot_ids, bin_group * share_size, share_size, 1)
    own_counts = lax.dynamic_slice_in_dim(obs_count, bin_group * share_size, share_size, 0)
    own_weights = point_weights(
        obs_wide, own_slots, own_counts, first_point + bin_group * share_size
    )
    ensemble_mixing_coefficients = gather_directly(own_weights, "bins", 2)
    return combine_ensemble_coefficients(prior_ensemble_densities, ensemble_mixing_coefficients)


def solution(mesh):
    placed = (
        P("bins", None, "space"),
        P(None, "space"),
        P(None, "bins"),
        P("space"),
        P("space"),
        P("space"),
        P("space"),
        P(None, "space"),
        P("space"),
    )
    return jax.shard_map(
        per_device, mesh=mesh, in_specs=placed, out_specs=P("bins", None, "space"), check_vma=False
    )
```

profile of v0, /device:TPU:7, one launch (start us, length us, event | category | flops | bytes accessed | tf_op | source)
XLA Modules:
  0.0 141.4 jit_solution(13482304723027759414)
XLA Ops:
  0.0 4.6 %copy.61 = bf16[48,32,256]{0,1,2:T(8,128)(2,1)S(1)} copy(bf16[48,32,256]{2,1,0:T(8,128)(2,1)} %param.11) | data formatting | bytes 1572864 | tf_op args[0]
  4.6 3.2 %collective-permute-start = (bf16[48,32,32]{0,1,2:T(8,128)(2,1)S(1)}, bf16[48,32,32]{0,1,2:T(8,128)(2,1)S(1)}, u32[]{:S(2)}, u32[]{:S(2)}) collective-permute-start(bf16[48,32,32]{0,1,2:T(8,128)(2,1)S(1)} %get-tuple-element.62), channel_id=1, source_target_pairs={{0,16},{16,32},{32,48},{48,64},{64,80},{80,96},{96,112},{112,128},... | collective-permute-start | bytes 294920 | tf_op jit(solution)/shard_map/ppermute | solution.py:24
  7.9 4.2 %collective-permute-start.1 = (bf16[48,32,32]{0,1,2:T(8,128)(2,1)S(1)}, bf16[48,32,32]{0,1,2:T(8,128)(2,1)S(1)}, u32[]{:S(2)}, u32[]{:S(2)}) collective-permute-start(bf16[48,32,32]{0,1,2:T(8,128)(2,1)S(1)} %get-tuple-element.63), channel_id=1, source_target_pairs={{16,0},{32,16},{48,32},{64,48},{80,64},{96,80},{112,96},{128,112},... | collective-permute-start | bytes 294920 | tf_op jit(solution)/shard_map/ppermute | solution.py:26
  12.1 0.7 compare_and_fusion
  12.8 0.7 compare_convert_fusion
  13.5 0.8 broadcast_compare_fusion
  14.4 0.9 fusion.20
  15.3 0.5 collective-permute-done
  15.8 0.9 collective-permute-done.1
  16.7 7.8 %convert_reduce_fusion = (f32[48,256]{0,1:T(8,128)S(1)}, bf16[48,32,256]{0,1,2:T(8,128)(2,1)}) fusion(f32[256]{0:T(256)S(1)} %bitcast.88, bf16[48,32,32]{0,1,2:T(8,128)(2,1)S(1)} %collective-permute-done.1, bf16[48,32,256]{0,1,2:T(8,128)(2,1)S(1)} %copy.61, f32[256]{0:T(256)S(1)} %bitcast.89, bf16[48,32,32]{0,1,2:T(8,128)(2,1)S(1)} %collective-permute-done, ...), kind=kLoop, calls=%fused_computation.12 | loop fusion | flops 9424896 | bytes 1823200 | tf_op jit(solution)/shard_map/reduce_sum | solution.py:153
  24.5 2.2 %gather_fusion = bf16[64,48,32]{1,2,0:T(8,128)(2,1)S(1)} fusion(bf16[48,32,256]{0,1,2:T(8,128)(2,1)} %get-tuple-element.57, s32[1024]{0:T(1024)S(1)} %pad_clamp_fusion.1), kind=kCustom, calls=%fused_computation | custom fusion | bytes 393472 | tf_op jit(solution)/shard_map/jit(_take)/gather | solution.py:184
  26.7 0.5 multiply_reduce_fusion
  27.3 0.8 reshape.201
  28.1 12.2 %all-to-all-start = ((f32[16,1,2048]{2,1,0:T(1,128)}), f32[16,1,2048]{2,1,0:T(1,128)S(1)}, u32[]{:S(2)}, u32[]{:S(2)}) async-start(f32[16,1,2048]{2,1,0:T(1,128)} %reshape.201), calls=%async_computation | async-start | bytes 262144 | tf_op jit(solution)/shard_map/all_to_all | solution.py:35
  40.4 9.1 %all-to-all-done = f32[16,1,2048]{2,1,0:T(1,128)S(1)} async-done(((f32[16,1,2048]{2,1,0:T(1,128)}), f32[16,1,2048]{2,1,0:T(1,128)S(1)}, u32[]{:S(2)}, u32[]{:S(2)}) %all-to-all-start) | async-done | bytes 131104 | tf_op jit(solution)/shard_map/all_to_all | solution.py:35
  49.5 0.5 broadcast.359
  50.0 1.0 reduce.3
  51.2 6.2 %collective-permute-start.3 = (f32[35,64]{1,0:T(8,128)S(1)}, f32[35,64]{1,0:T(8,128)S(1)}, u32[]{:S(2)}, u32[]{:S(2)}) collective-permute-start(f32[35,64]{1,0:T(8,128)S(1)} %pad_maximum_fusion.3), channel_id=1, source_target_pairs={{16,0},{32,16},{48,32},{64,48},{80,64},{96,80},{112,96},{128,112},... | collective-permute-start | bytes 26888 | tf_op jit(solution)/shard_map/ppermute | solution.py:26
  57.4 1.9 %collective-permute-start.2 = (f32[35,64]{1,0:T(8,128)S(1)}, f32[35,64]{1,0:T(8,128)S(1)}, u32[]{:S(2)}, u32[]{:S(2)}) collective-permute-start(f32[35,64]{1,0:T(8,128)S(1)} %pad_maximum_fusion.3), channel_id=1, source_target_pairs={{0,16},{16,32},{32,48},{48,64},{64,80},{80,96},{96,112},{112,128},... | collective-permute-start | bytes 26888 | tf_op jit(solution)/shard_map/ppermute | solution.py:24
  59.6 4.5 %collective-permute-done.2 = f32[35,64]{1,0:T(8,128)S(1)} collective-permute-done((f32[35,64]{1,0:T(8,128)S(1)}, f32[35,64]{1,0:T(8,128)S(1)}, u32[]{:S(2)}, u32[]{:S(2)}) %collective-permute-start.2) | collective-permute-done | bytes 8992 | tf_op jit(solution)/shard_map/ppermute | solution.py:24
  64.2 0.1 copy.67
  64.3 1.0 gather_fusion.1
  65.3 0.2 copy.68
  65.6 0.1 compare_select_fusion
  65.7 0.5 fusion.13
  66.2 0.7 multiply_reduce_fusion.1
  67.0 0.1 copy.69
  67.2 13.0 %while.13 = (s32[]{:T(128)}, f32[16,32,32]{1,2,0:T(8,128)S(1)}, f32[16,32,32]{2,1,0:T(8,128)S(1)}, s32[]{:T(128)}) while((s32[]{:T(128)}, f32[16,32,32]{1,2,0:T(8,128)S(1)}, f32[16,32,32]{2,1,0:T(8,128)S(1)}, s32[]{:T(128)}) %tuple.41), condition=%wide.region_5.6_spmd.clone, body=%wide.region_4.5_spmd.clone.sunk | while | flops 18909184 | bytes 860213 | solution.py:127
  67.3 0.5 fusion.66
  67.8 0.4 fusion.67
  68.2 0.6 convolution_bitcast_fusion.3
  68.9 0.5 fusion.66
  69.5 0.4 fusion.67
  69.8 0.6 convolution_bitcast_fusion.3
  70.5 0.5 fusion.66
  71.1 0.4 fusion.67
  71.5 0.6 convolution_bitcast_fusion.3
  72.2 0.5 fusion.66
  72.7 0.4 fusion.67
  73.1 0.6 convolution_bitcast_fusion.3
  73.8 0.5 fusion.66
  74.3 0.4 fusion.67
  74.7 0.6 convolution_bitcast_fusion.3
  75.4 0.5 fusion.66
  76.0 0.4 fusion.67
  76.3 0.6 convolution_bitcast_fusion.3
  77.0 0.5 fusion.66
  77.6 0.4 fusion.67
  78.0 0.6 convolution_bitcast_fusion.3
  78.7 0.5 fusion.66
  79.2 0.4 fusion.67
  79.6 0.6 convolution_bitcast_fusion.3
  80.2 0.6 convolution_bitcast_fusion.1
  80.8 0.6 fusion.36
  81.4 0.2 add_bitcast_fusion
  81.6 0.1 copy.70
  81.7 2.5 %broadcast_bitcast_fusion = f32[16,16,32,32]{3,2,1,0:T(8,128)} fusion(f32[32,32,16]{0,1,2:T(8,128)S(1)} %copy.70), kind=kLoop, calls=%fused_computation.106 | loop fusion | bytes 1114112
  84.2 4.7 %reshape.203 = f32[16,1,16384]{2,1,0:T(1,128)} reshape(f32[16,16,32,32]{3,2,1,0:T(8,128)} %broadcast_bitcast_fusion) | data formatting | bytes 2097152
  88.9 5.2 %all-to-all-start.1 = ((f32[16,1,16384]{2,1,0:T(1,128)}), f32[16,1,16384]{2,1,0:T(1,128)}, u32[]{:S(2)}, u32[]{:S(2)}) async-start(f32[16,1,16384]{2,1,0:T(1,128)} %reshape.203), calls=%async_computation.1 | async-start | bytes 2097152 | tf_op jit(solution)/shard_map/all_to_all | solution.py:35
  94.1 28.1 %all-to-all-done.1 = f32[16,1,16384]{2,1,0:T(1,128)} async-done(((f32[16,1,16384]{2,1,0:T(1,128)}), f32[16,1,16384]{2,1,0:T(1,128)}, u32[]{:S(2)}, u32[]{:S(2)}) %all-to-all-start.1) | async-done | bytes 1048608 | tf_op jit(solution)/shard_map/all_to_all | solution.py:35
  122.2 4.5 %reduce.4 = f32[16,16384]{1,0:T(8,128)S(1)} reduce(f32[16,1,16384]{2,1,0:T(1,128)} %all-to-all-done.1, f32[]{:T(128)} %broadcast.359), dimensions={1}, to_apply=%all_to_all.7.reduce_sub_computation | reduce | bytes 2097156 | tf_op jit(solution)/shard_map/all_to_all | solution.py:35
  126.7 2.7 %reshape.204 = f32[16,16,32,32]{3,2,1,0:T(8,128)} reshape(f32[16,16384]{1,0:T(8,128)S(1)} %reduce.4) | data formatting | bytes 2097152
  129.4 7.4 %fusion.8 = bf16[48,32,256]{0,1,2:T(8,128)(2,1)} fusion(f32[32,32,256]{0,1,2:T(8,128)} %bitcast.79, bf16[48,32,256]{0,1,2:T(8,128)(2,1)S(1)} %copy-done.1, f32[48,256]{0,1:T(8,128)S(1)} %broadcast_multiply_fusion), kind=kOutput, calls=%fused_computation.19 | convolution fusion | flops 152567808 | bytes 2670592 | tf_op jit(solution)/shard_map/bin,imn->bmn/dot_general | solution.py:155
  136.8 4.6 %copy.71 = bf16[48,32,256]{2,1,0:T(8,128)(2,1)} copy(bf16[48,32,256]{0,1,2:T(8,128)(2,1)} %fusion.8) | data formatting | bytes 1572864 | tf_op jit(solution)/shard_map/convert_element_type | solution.py:158
  (63 shorter events, 1.4 us)
Async XLA Ops:
  0.0 14.4 %copy-start = (f32[16,48]{1,0:T(8,128)S(1)}, f32[16,48]{1,0:T(8,128)}, u32[]{:S(2)}) copy-start(f32[16,48]{1,0:T(8,128)} %param.13) | copy-start | bytes 9220
  4.6 35.8 %copy-start.2 = (s32[64]{0:T(128)S(1)}, s32[64]{0:T(128)}, u32[]{:S(2)}) copy-start(s32[64]{0:T(128)} %param.14) | copy-start | bytes 772
  4.6 11.2 %collective-permute-start = (bf16[48,32,32]{0,1,2:T(8,128)(2,1)S(1)}, bf16[48,32,32]{0,1,2:T(8,128)(2,1)S(1)}, u32[]{:S(2)}, u32[]{:S(2)}) collective-permute-start(bf16[48,32,32]{0,1,2:T(8,128)(2,1)S(1)} %get-tuple-element.62), channel_id=1, source_target_pairs={{0,16},{16,32},{32,48},{48,64},{64,80},{80,96},{96,112},{112,128},... | collective-permute-start | bytes 294920 | tf_op jit(solution)/shard_map/ppermute | solution.py:24
  7.8 43.3 %copy-start.3 = (f32[64]{0:T(128)S(1)}, f32[64]{0:T(128)}, u32[]{:S(2)}) copy-start(f32[64]{0:T(128)} %param.17) | copy-start | bytes 772
  7.8 43.3 %copy-start.4 = (f32[64]{0:T(128)S(1)}, f32[64]{0:T(128)}, u32[]{:S(2)}) copy-start(f32[64]{0:T(128)} %param.16) | copy-start | bytes 772
  7.9 8.8 %collective-permute-start.1 = (bf16[48,32,32]{0,1,2:T(8,128)(2,1)S(1)}, bf16[48,32,32]{0,1,2:T(8,128)(2,1)S(1)}, u32[]{:S(2)}, u32[]{:S(2)}) collective-permute-start(bf16[48,32,32]{0,1,2:T(8,128)(2,1)S(1)} %get-tuple-element.63), channel_id=1, source_target_pairs={{16,0},{32,16},{48,32},{64,48},{80,64},{96,80},{112,96},{128,112},... | collective-permute-start | bytes 294920 | tf_op jit(solution)/shard_map/ppermute | solution.py:26
  13.5 45.9 %copy-start.5 = (s32[256]{0:T(256)S(1)}, s32[256]{0:T(256)}, u32[]{:S(2)}) copy-start(s32[256]{0:T(256)} %param.19) | copy-start | bytes 3076
  28.1 21.4 %all-to-all-start = ((f32[16,1,2048]{2,1,0:T(1,128)}), f32[16,1,2048]{2,1,0:T(1,128)S(1)}, u32[]{:S(2)}, u32[]{:S(2)}) async-start(f32[16,1,2048]{2,1,0:T(1,128)} %reshape.201), calls=%async_computation | async-start | bytes 262144 | tf_op jit(solution)/shard_map/all_to_all | solution.py:35
  51.2 8.3 %collective-permute-start.3 = (f32[35,64]{1,0:T(8,128)S(1)}, f32[35,64]{1,0:T(8,128)S(1)}, u32[]{:S(2)}, u32[]{:S(2)}) collective-permute-start(f32[35,64]{1,0:T(8,128)S(1)} %pad_maximum_fusion.3), channel_id=1, source_target_pairs={{16,0},{32,16},{48,32},{64,48},{80,64},{96,80},{112,96},{128,112},... | collective-permute-start | bytes 26888 | tf_op jit(solution)/shard_map/ppermute | solution.py:26
  57.4 6.6 %collective-permute-start.2 = (f32[35,64]{1,0:T(8,128)S(1)}, f32[35,64]{1,0:T(8,128)S(1)}, u32[]{:S(2)}, u32[]{:S(2)}) collective-permute-start(f32[35,64]{1,0:T(8,128)S(1)} %pad_maximum_fusion.3), channel_id=1, source_target_pairs={{0,16},{16,32},{32,48},{48,64},{64,80},{80,96},{96,112},{112,128},... | collective-permute-start | bytes 26888 | tf_op jit(solution)/shard_map/ppermute | solution.py:24
  88.9 33.2 %all-to-all-start.1 = ((f32[16,1,16384]{2,1,0:T(1,128)}), f32[16,1,16384]{2,1,0:T(1,128)}, u32[]{:S(2)}, u32[]{:S(2)}) async-start(f32[16,1,16384]{2,1,0:T(1,128)} %reshape.203), calls=%async_computation.1 | async-start | bytes 2097152 | tf_op jit(solution)/shard_map/all_to_all | solution.py:35
  94.1 35.3 %copy-start.1 = (bf16[48,32,256]{0,1,2:T(8,128)(2,1)S(1)}, bf16[48,32,256]{0,1,2:T(8,128)(2,1)}, u32[]{:S(2)}) copy-start(bf16[48,32,256]{0,1,2:T(8,128)(2,1)} %get-tuple-element.57) | copy-start | bytes 2359300
where the time goes:
time: 142 us; the launch traced here: 141 us
  waiting for transfers between devices  43.1 us (30%)
  starting transfers between devices  32.9 us (23%)
  local copies, waits for them, and re-layouts  25.1 us (18%)
  matrix products  22.9 us (16%)
  other arithmetic  16.7 us (12%)
    all_to_all x2, waiting for transfers between devices, from_everyone(): lax.all_to_all(jnp.broadcast_to(value[None], (count, *value.shape)), axis...  37.2 us
    all_to_all x2, starting transfers between devices, from_everyone(): lax.all_to_all(jnp.broadcast_to(value[None], (count, *value.shape)), axis...  17.4 us
    unnamed x19, local copies, waits for them, and re-layouts  15.6 us
    ppermute x2, starting transfers between devices, with_halo(): lax.ppermute(head, axis, [((i + 1) % count, i) for i in range(ends)])  10.4 us
    reduce_sum x1, other arithmetic, combine_ensemble_coefficients(): ens_mean = jnp.mean(swell_variance_density, axis=1, keepdims=True)  7.78 us
    dot_general x1, matrix products, combine_ensemble_coefficients(): jnp.einsum('bin,imn->bmn', anomaly, ensemble_mixing_coefficients, precisi...  7.4 us
    all_to_all x2, other arithmetic, from_everyone(): lax.all_to_all(jnp.broadcast_to(value[None], (count, *value.shape)), axis...  5.49 us
    ppermute x2, starting transfers between devices, with_halo(): lax.ppermute(tail, axis, [(i, (i + 1) % count) for i in range(ends)])  5.13 us
  transfers between devices with their start and end apart: 6, of which 5 were waited for; matrix products, arithmetic and copies ran while one was open for 2% of the time, Pallas kernels for 0%

commit v1 on v0

v1 whole, which is shorter than its diff:
```python
import functools
import math

import jax
import jax.numpy as jnp
import numpy as np
from jax import lax
from jax.experimental import pallas as pl
from jax.experimental.pallas import tpu as pltpu
from jax.sharding import PartitionSpec as P

ND = 24
ROWS = 32
LOC_R = 6
NS_ITERS = 8
COURANT_MAX = 0.7
FREQ_RATIO = 1.1

BINS = 48
MEM = 32
PTS = 256
OBS = 64
NEAR = 3 * OBS
OWN = 16
GROUPS = 2 * OWN
TILES = 32
ZC = 8
SIX = 6
WEST = ((0, 0), (0, 3), (1, 0), (1, 3))
EAST = ((0, 1), (0, 2), (1, 1), (1, 2))

MESH = pl.DeviceIdType.MESH
F32 = jnp.float32
BF16 = jnp.bfloat16


def iota(shape, dim):
    return lax.broadcasted_iota(jnp.int32, shape, dim)


def dot(a, b):
    return jnp.dot(a, b, preferred_element_type=F32)


def split(a):
    high = a.astype(BF16)
    return high, (a - high.astype(F32)).astype(BF16)


def stacked(a):
    return jnp.concatenate(split(a), axis=0)


def folded(a):
    half = a.shape[0] // 2
    return a[:half] + a[half:]


def block_diagonal(rows, mask):
    return jnp.concatenate([rows.astype(BF16)] * 8, axis=0) * mask


def lanes_roll(a, by):
    return pltpu.roll(a, by % 128, 1)


def exchange_kernel(
    cos_ref, sin_ref, x_ref, nb_ref, opw_ref, opt_ref, oty_ref, oval_ref, ovar_ref, olist_ref, ocnt_ref,
    l_ref, t_ref,
    a1, a2, a3, send_w, send_e, recv_w, recv_e, meta, meta_l, meta_r, fore, sums, core_in, chip_sum, z_in,
    total, total_l, total_r, relay, w8, expand, m_s, z_s, g_s, ssem, rsem,
):
    tile = lax.axis_index("space")
    me = lax.axis_index("bins")
    core = me % 2
    left, right = (tile + TILES - 1) % TILES, (tile + 1) % TILES
    mate = me + 1 - 2 * core

    barrier = pltpu.get_barrier_semaphore()
    partners = [(left, me), (right, me), (tile, mate)]
    partners += [(tile, (me + 2 * k) % (2 * ZC)) for k in (4, 3, 5, 2, 6, 1, 7)]
    for who in partners:
        pl.semaphore_signal(barrier, inc=1, device_id=who, device_id_type=MESH)

    def copy(src, dst, n, who):
        return pltpu.make_async_remote_copy(
            src_ref=src, dst_ref=dst, send_sem=ssem.at[n], recv_sem=rsem.at[n], device_id=who, device_id_type=MESH
        )

    lane = iota((MEM, 128), 1)
    block = lane // 32

    def pack(j, _):
        for bins, buf, half, at in ((WEST, send_w, 1, 96), (EAST, send_e, 0, 0)):
            out = None
            for k, (f, q) in enumerate(bins):
                edge = x_ref[f * ND + q * SIX + j, :, 128 * half : 128 * half + 128].astype(F32)
                edge = lanes_roll(edge, 32 * k - at)
                out = edge if out is None else jnp.where(block == k, edge, out)
            buf[j] = out.astype(BF16)
        return 0

    lax.fori_loop(0, SIX, pack, 0)

    zeros = jnp.zeros((1, OBS), F32)
    point = opt_ref[...]
    rows = [
        (point // ROWS).astype(F32), (point % ROWS).astype(F32), oval_ref[...], lax.rsqrt(ovar_ref[...]),
        zeros, zeros, zeros, zeros,
    ]
    packed = jnp.concatenate(rows, axis=0)
    meta[...] = jnp.concatenate([packed, jnp.zeros((8, OBS), F32)], axis=1)

    freq = (jnp.where(iota((BINS, PTS), 0) >= ND, 1, 0) + 2 * me).astype(F32)
    speed = COURANT_MAX * jnp.exp(-freq * math.log(FREQ_RATIO))
    open_side = (nb_ref[...] >= 0).astype(F32)
    cosine, sine = cos_ref[...], sin_ref[...]
    cx, cy = speed * jnp.abs(cosine), speed * jnp.abs(sine)
    a1[...] = 1.0 - cx - cy
    a2[...] = cx * jnp.where(cosine > 0, open_side[0:1], open_side[1:2])
    a3[...] = cy * jnp.where(sine > 0, open_side[2:3], open_side[3:4])

    here = (iota((PTS, OBS), 0) == point - tile * PTS).astype(BF16)
    kinds = (iota((16, OBS), 0) == oty_ref[...]).astype(F32)
    weights = lax.dot_general(
        opw_ref[...], kinds, (((0,), (0,)), ((), ())), precision=lax.Precision.HIGHEST, preferred_element_type=F32
    )

    pl.semaphore_wait(barrier, len(partners))
    halo = [
        copy(send_w, recv_w, 0, (right, me)),
        copy(send_e, recv_e, 1, (left, me)),
        copy(meta, meta_l, 2, (right, me)),
        copy(meta, meta_r, 3, (left, me)),
    ]
    for c in halo:
        c.start()

    ids = jnp.where(iota((MEM, PTS), 0) < ocnt_ref[...], olist_ref[...] - (tile - 1) * OBS, -1)
    ids = jnp.where(olist_ref[...] >= 0, ids, -1)
    low, high = ids[:, :128], ids[:, 128:]
    low = jnp.where(core == 0, low, lanes_roll(low, -32))
    high = jnp.where(core == 0, high, lanes_roll(high, -32))
    ids = jnp.where(
        block == 0, low, jnp.where(block == 1, lanes_roll(low, -32), jnp.where(block == 2, lanes_roll(high, 64), lanes_roll(high, 32)))
    )
    number = iota((NEAR, 128), 0)
    used = jnp.zeros((NEAR, 128), F32)
    for slot in range(MEM):
        used = jnp.where(ids[slot : slot + 1] == number, 1.0, used)

    for c in halo:
        c.wait_recv()

    def propagate(j, _):
        w_in = recv_w[j].astype(F32)
        e_in = recv_e[j].astype(F32)
        for f in range(2):
            for q in range(4):
                b = f * ND + q * SIX + j
                xl = x_ref[b, :, 0:128].astype(F32)
                xr = x_ref[b, :, 128:256].astype(F32)
                if (f, q) in WEST:
                    edge = lanes_roll(w_in, -32 * WEST.index((f, q)))
                    near, far = lanes_roll(xl, 32), lanes_roll(xr, 32)
                    ixl = jnp.where(block == 0, edge, near)
                    ixr = jnp.where(block == 0, near, far)
                else:
                    edge = lanes_roll(e_in, 96 - 32 * EAST.index((f, q)))
                    near, far = lanes_roll(xl, 96), lanes_roll(xr, 96)
                    ixl = jnp.where(block == 3, far, near)
                    ixr = jnp.where(block == 3, edge, far)
                turn = 1 if q < 2 else 127
                iyl, iyr = lanes_roll(xl, turn), lanes_roll(xr, turn)
                r1, r2, r3 = a1[pl.ds(b, 1), :], a2[pl.ds(b, 1), :], a3[pl.ds(b, 1), :]
                fore[b, :, 0:128] = (xl * r1[:, :128] + ixl * r2[:, :128] + iyl * r3[:, :128]).astype(BF16)
                fore[b, :, 128:256] = (xr * r1[:, 128:] + ixr * r2[:, 128:] + iyr * r3[:, 128:]).astype(BF16)
        return 0

    lax.fori_loop(0, SIX, propagate, 0)

    predicted = jnp.zeros((MEM, OBS), F32)
    for part in range(4):
        at = dot(fore[12 * part : 12 * part + 12].reshape(12 * MEM, PTS), here)
        for i in range(12):
            b = 12 * part + i
            predicted += at[MEM * i : MEM * (i + 1)] * weights[b : b + 1]
    sums[...] = jnp.concatenate([predicted[:16], predicted[16:]], axis=1)
    pair = copy(sums, core_in, 4, (tile, mate))
    pair.start()

    metas = jnp.concatenate(
        [
            jnp.where(iota((8, 128), 1) < OBS, meta_l[...], lanes_roll(meta[...], 64)),
            jnp.where(iota((8, 128), 1) < OBS, meta_r[...], 0.0),
        ],
        axis=1,
    )
    places = jnp.concatenate([metas, jnp.zeros((120, PTS), F32)], axis=0).T
    own_lane = iota((NEAR, 128), 1)
    col = (tile * 8 + 2 * (own_lane // 32) + core).astype(F32)
    row = (own_lane % 32).astype(F32)
    distance = (places[:NEAR, 0:1] - col) ** 2 + (places[:NEAR, 1:2] - row) ** 2
    taper = (1.0 - distance / (2.0 * LOC_R * LOC_R)) ** 2 * used
    taper_high, taper_low = split(taper)

    pair.wait_recv()
    chip_sum[...] = sums[...] + core_in[...]
    far = [copy(chip_sum, z_in.at[k - 1], 4 + k, (tile, (me + 2 * k) % (2 * ZC))) for k in (4, 3, 5, 2, 6, 1, 7)]
    for c in far:
        c.start()

    big_lane = iota((128, PTS), 1)
    target = 32 * ((big_lane // 32) % 4) + big_lane // 128
    source = iota((128, PTS), 0)
    for g in range(OWN):
        spread = (source == target + 2 * g).astype(BF16)
        expand[g] = spread
        w8[g] = dot(taper_high, spread).astype(BF16)

    def turn_in(i, _):
        f0, f1 = fore[2 * i].astype(F32), fore[2 * i + 1].astype(F32)
        parts = []
        for q in range(4):
            h = q // 2
            c0, c1 = f0[:, 128 * h : 128 * h + 128], f1[:, 128 * h : 128 * h + 128]
            if q % 2 == 0:
                parts.append(jnp.where(lane < 64, c0, lanes_roll(c1, 64)))
            else:
                parts.append(jnp.where(lane < 64, lanes_roll(c0, 64), c1))
        turned = jnp.concatenate(parts, axis=0).T
        relay[pl.ds(2 * i, 64, stride=BINS), :] = turned[:64]
        relay[pl.ds(2 * i + 1, 64, stride=BINS), :] = turned[64:]
        return 0

    lax.fori_loop(0, BINS // 2, turn_in, 0)

    for c in far:
        c.wait_recv()
    acc = chip_sum[...]
    for k in range(7):
        acc += z_in[k]
    total[...] = acc
    beside = [copy(total, total_l, 12, (right, me)), copy(total, total_r, 13, (left, me))]
    for c in beside:
        c.start()

    def to_operand(g, _):
        two = [relay[pl.ds(pl.multiple_of((2 * g + h) * BINS, 8), BINS), :] for h in range(2)]
        l_ref[g] = jnp.concatenate(two, axis=1).astype(BF16)
        return 0

    lax.fori_loop(0, GROUPS, to_operand, 0)
    for c in beside:
        c.wait_recv()

    half = iota((16, 128), 1) < OBS
    pl_, po, pr = total_l[...], total[...], total_r[...]
    first = jnp.where(half, pl_, lanes_roll(po, 64)), jnp.where(half, pr, 0.0)
    second = jnp.where(half, lanes_roll(pl_, 64), po), jnp.where(half, lanes_roll(pr, 64), 0.0)
    seen = jnp.concatenate([jnp.concatenate(first, axis=1), jnp.concatenate(second, axis=1)], axis=0)
    mean = jnp.sum(seen, axis=0, keepdims=True) * (1.0 / MEM)
    anomaly = (seen - mean) * metas[3:4]
    innovation = (metas[2:3] - mean) * metas[3:4]
    pulled = (anomaly * innovation)[:, :NEAR] * (1.0 / (MEM - 1))
    pull = folded(dot(stacked(pulled), taper_high)) + dot(pulled.astype(BF16), taper_low)
    pulls = stacked(pull)
    y_t = jnp.concatenate([anomaly] * 4, axis=0).T[:NEAR]
    y_t = jnp.concatenate([y_t, y_t], axis=1).astype(BF16)
    y = anomaly[:, :NEAR].astype(BF16)

    eye = (iota((MEM, PTS), 0) == iota((MEM, PTS), 1) % MEM).astype(F32)
    same = (iota((PTS, PTS), 0) // MEM == iota((PTS, PTS), 1) // MEM).astype(BF16)
    squares = []
    for g in range(OWN):
        matrix = eye + dot(y, w8[g] * y_t) * (1.0 / (MEM - 1))
        m_s[g] = matrix
        squares.append(jnp.sum(matrix * matrix, axis=0, keepdims=True))
        g_s[g] = folded(dot(pulls, expand[g]))
    norm = folded(dot(stacked(jnp.concatenate(squares, axis=0)), same))
    inv_scale = lax.rsqrt(norm)
    root_scale = jnp.sqrt(inv_scale)

    for it in range(NS_ITERS):
        for g in range(OWN):
            current = m_s[g] * inv_scale[g : g + 1] if it == 0 else m_s[g]
            step = 0.5 * (eye - current)
            operand = block_diagonal(step, same)
            if it == 0:
                moved = current + dot(current.astype(BF16), operand)
                z_s[g] = eye + step
            elif it == NS_ITERS - 1:
                inverse = z_s[g]
                z_s[g] = inverse + dot(inverse.astype(BF16), operand)
                continue
            else:
                inverse = z_s[g]
                both = dot(jnp.concatenate([current, inverse], axis=0).astype(BF16), operand)
                moved = current + both[:MEM]
                z_s[g] = inverse + both[MEM:]
            m_s[g] = moved + dot(moved.astype(BF16), operand)

    swaps = []
    for g in range(OWN):
        root = z_s[g] * root_scale[g : g + 1]
        half_step = jnp.sum(root * g_s[g], axis=0, keepdims=True)
        shift = folded(dot(stacked(root * half_step), same))
        mix = root + shift
        mix = mix + (1.0 - jnp.sum(mix, axis=0, keepdims=True)) * (1.0 / MEM)
        t_ref[core * OWN + g] = mix.astype(BF16)
        if g % 4 == 3:
            part = t_ref.at[pl.ds(core * OWN + g - 3, 4)]
            swap = copy(part, part, 14 + g // 4, (tile, mate))
            swap.start()
            swaps.append(swap)
    for c in swaps:
        c.wait()
    for c in halo + [pair] + far + beside:
        c.wait_send()


def combine_kernel(l_ref, t_ref, out_ref, relay):
    same = (iota((PTS, PTS), 0) // MEM == iota((PTS, PTS), 1) // MEM).astype(BF16)
    for g in range(GROUPS):
        mixed = dot(l_ref[g], block_diagonal(t_ref[g], same))
        for h in range(2):
            relay[(2 * g + h) * BINS : (2 * g + h + 1) * BINS, :] = mixed[:, 128 * h : 128 * h + 128]
    lane = iota((MEM, 128), 1)
    for i in range(BINS // 2):
        two = [relay[pl.ds(2 * i + k, 64, stride=BINS), :] for k in range(2)]
        turned = jnp.concatenate(two, axis=0).T
        q = [turned[MEM * k : MEM * (k + 1)] for k in range(4)]
        for h in range(2):
            a, b = q[2 * h], q[2 * h + 1]
            cut = slice(128 * h, 128 * h + 128)
            out_ref[2 * i, :, cut] = jnp.where(lane < 64, a, lanes_roll(b, 64)).astype(BF16)
            out_ref[2 * i + 1, :, cut] = jnp.where(lane < 64, lanes_roll(a, 64), b).astype(BF16)


def per_device(x, neighbors, obs_operator, obs_point, obs_type, obs_value, obs_var, obs_list, obs_count):
    theta = 2.0 * np.pi * (np.arange(BINS) % ND + 0.5) / ND
    cosine = jnp.asarray(np.broadcast_to(np.cos(theta)[:, None], (BINS, PTS)), F32)
    sine = jnp.asarray(np.broadcast_to(np.sin(theta)[:, None], (BINS, PTS)), F32)
    vmem = pl.BlockSpec(memory_space=pltpu.VMEM)
    tile_f32 = pltpu.VMEM((16, 128), F32)
    operand, transform = pl.pallas_call(
        exchange_kernel,
        out_shape=(
            jax.ShapeDtypeStruct((GROUPS, BINS, PTS), BF16),
            jax.ShapeDtypeStruct((GROUPS, MEM, PTS), BF16),
        ),
        in_specs=[vmem] * 11,
        out_specs=(vmem, vmem),
        scratch_shapes=[
            pltpu.VMEM((BINS, PTS), F32),
            pltpu.VMEM((BINS, PTS), F32),
            pltpu.VMEM((BINS, PTS), F32),
            pltpu.VMEM((SIX, MEM, 128), BF16),
            pltpu.VMEM((SIX, MEM, 128), BF16),
            pltpu.VMEM((SIX, MEM, 128), BF16),
            pltpu.VMEM((SIX, MEM, 128), BF16),
            pltpu.VMEM((8, 128), F32),
            pltpu.VMEM((8, 128), F32),
            pltpu.VMEM((8, 128), F32),
            pltpu.VMEM((BINS, MEM, PTS), BF16),
            tile_f32,
            tile_f32,
            tile_f32,
            pltpu.VMEM((7, 16, 128), F32),
            tile_f32,
            tile_f32,
            tile_f32,
            pltpu.VMEM((64 * BINS, 128), F32),
            pltpu.VMEM((OWN, NEAR, PTS), BF16),
            pltpu.VMEM((OWN, 128, PTS), BF16),
            pltpu.VMEM((OWN, MEM, PTS), F32),
            pltpu.VMEM((OWN, MEM, PTS), F32),
            pltpu.VMEM((OWN, MEM, PTS), F32),
            pltpu.SemaphoreType.DMA((18,)),
            pltpu.SemaphoreType.DMA((18,)),
        ],
        compiler_params=pltpu.CompilerParams(
            collective_id=0, has_side_effects=True, vmem_limit_bytes=40 << 20
        ),
        name="exchange",
    )(
        cosine, sine, x, neighbors, obs_operator, obs_point[None], obs_type[None], obs_value[None], obs_var[None],
        obs_list, obs_count[None],
    )
    return pl.pallas_call(
        combine_kernel,
        out_shape=jax.ShapeDtypeStruct((BINS, MEM, PTS), BF16),
        in_specs=[vmem, vmem],
        out_specs=vmem,
        scratch_shapes=[pltpu.VMEM((64 * BINS, 128), F32)],
        compiler_params=pltpu.CompilerParams(vmem_limit_bytes=40 << 20),
        name="combine",
    )(operand, transform)


def solution(mesh):
    placed = (
        P("bins", None, "space"),
        P(None, "space"),
        P(None, "bins"),
        P("space"),
        P("space"),
        P("space"),
        P("space"),
        P(None, "space"),
        P("space"),
    )
    return jax.shard_map(
        per_device, mesh=mesh, in_specs=placed, out_specs=P("bins", None, "space"), check_vma=False
    )
```

time: 142 us -> 48.4 us (0.34)
  the two profiles are of different devices: /device:TPU:7 before, /device:TPU:1 now
where the time goes in v1:
time: 48.4 us; the launch traced here: 48 us
  Pallas kernels  40.5 us (84%)
  local copies, waits for them, and re-layouts  7.49 us (15%)
    pallas_call x1, Pallas kernels, per_device(): pl.pallas_call(exchange_kernel, out_shape=(jax.ShapeDtypeStruct((GROUPS,...  37.9 us
    unnamed x22, local copies, waits for them, and re-layouts  7.49 us
    pallas_call x1, Pallas kernels, per_device(): pl.pallas_call(combine_kernel, out_shape=jax.ShapeDtypeStruct((BINS, MEM,...  2.58 us

profile of v1, /device:TPU:1, one launch (start us, length us, event | category | flops | bytes accessed | tf_op | source)
XLA Modules:
  0.0 48.0 jit_solution(15775430694639445203)
XLA Ops:
  0.0 0.0 copy-start.4
  0.0 0.0 copy-start.6
  0.0 0.7 %copy-done.4 = f32[16,48]{1,0:T(8,128)S(1)} copy-done((f32[16,48]{1,0:T(8,128)S(1)}, f32[16,48]{1,0:T(8,128)}, u32[]{:S(2)}) %copy-start.4) | copy-done | bytes 3096
  0.7 0.0 copy-done.6
  0.7 0.0 copy-start
  0.7 1.1 %copy-done = bf16[48,32,256]{2,1,0:T(8,128)(2,1)S(1)} copy-done((bf16[48,32,256]{2,1,0:T(8,128)(2,1)S(1)}, bf16[48,32,256]{2,1,0:T(8,128)(2,1)}, u32[]{:S(2)}) %copy-start) | copy-done | bytes 786456
  1.8 0.0 copy-start.1
  1.8 0.8 %copy-done.1 = f32[48,256]{1,0:T(8,128)S(1)} copy-done((f32[48,256]{1,0:T(8,128)S(1)}, f32[48,256]{1,0:T(8,128)}, u32[]{:S(2)}) %copy-start.1) | copy-done | bytes 49176
  2.6 0.0 copy-start.2
  2.6 0.8 %copy-done.2 = f32[48,256]{1,0:T(8,128)S(1)} copy-done((f32[48,256]{1,0:T(8,128)S(1)}, f32[48,256]{1,0:T(8,128)}, u32[]{:S(2)}) %copy-start.2) | copy-done | bytes 49176
  3.4 0.0 copy-start.3
  3.4 0.8 %copy-done.3 = s32[32,256]{1,0:T(8,128)S(1)} copy-done((s32[32,256]{1,0:T(8,128)S(1)}, s32[32,256]{1,0:T(8,128)}, u32[]{:S(2)}) %copy-start.3) | copy-done | bytes 32792
  4.2 0.0 copy-start.5
  4.2 0.7 %copy-done.5 = s32[4,256]{1,0:T(4,128)S(1)} copy-done((s32[4,256]{1,0:T(4,128)S(1)}, s32[4,256]{1,0:T(4,128)}, u32[]{:S(2)}) %copy-start.5) | copy-done | bytes 4120
  4.9 0.0 copy-start.7
  4.9 0.7 %copy-done.7 = s32[64]{0:T(128)S(1)} copy-done((s32[64]{0:T(128)S(1)}, s32[64]{0:T(128)}, u32[]{:S(2)}) %copy-start.7) | copy-done | bytes 280
  5.5 0.0 copy-start.8
  5.5 0.7 %copy-done.8 = s32[64]{0:T(128)S(1)} copy-done((s32[64]{0:T(128)S(1)}, s32[64]{0:T(128)}, u32[]{:S(2)}) %copy-start.8) | copy-done | bytes 280
  6.2 0.0 copy-start.9
  6.2 0.7 %copy-done.9 = f32[64]{0:T(128)S(1)} copy-done((f32[64]{0:T(128)S(1)}, f32[64]{0:T(128)}, u32[]{:S(2)}) %copy-start.9) | copy-done | bytes 280
  6.8 0.0 copy-start.10
  6.8 0.7 %copy-done.10 = f32[64]{0:T(128)S(1)} copy-done((f32[64]{0:T(128)S(1)}, f32[64]{0:T(128)}, u32[]{:S(2)}) %copy-start.10) | copy-done | bytes 280
  7.5 37.9 %exchange.1 = (bf16[32,48,256]{2,1,0:T(8,128)(2,1)S(1)}, bf16[32,32,256]{2,1,0:T(8,128)(2,1)S(1)}) custom-call(f32[48,256]{1,0:T(8,128)S(1)} %copy-done.2, f32[48,256]{1,0:T(8,128)S(1)} %copy-done.1, bf16[48,32,256]{2,1,0:T(8,128)(2,1)S(1)} %copy-done, s32[4,256]{1,0:T(4,128)S(1)} %copy-done.5, f32[16,48]{1,0:T(8,128)S(1)} %copy-done.4, ...), custom_call_target="tpu_custom_call" | custom-call | tf_op jit(solution)/shard_map/exchange/pallas_call | solution.py:346
  45.4 2.6 %combine.1 = bf16[48,32,256]{2,1,0:T(8,128)(2,1)} custom-call(bf16[32,48,256]{2,1,0:T(8,128)(2,1)S(1)} %get-tuple-element.7.l_ref, bf16[32,32,256]{2,1,0:T(8,128)(2,1)S(1)} %get-tuple-element.8.t_ref), custom_call_target="tpu_custom_call" | custom-call | tf_op jit(solution)/shard_map/combine/pallas_call | solution.py:390
Async XLA Ops:
  0.0 0.7 %copy-start.4 = (f32[16,48]{1,0:T(8,128)S(1)}, f32[16,48]{1,0:T(8,128)}, u32[]{:S(2)}) copy-start(f32[16,48]{1,0:T(8,128)} %opw_ref.1) | copy-start | bytes 9220
  0.0 0.7 %copy-start.6 = (s32[256]{0:T(256)S(1)}, s32[256]{0:T(256)}, u32[]{:S(2)}) copy-start(s32[256]{0:T(256)} %param.19) | copy-start | bytes 3076
  0.7 1.1 %copy-start = (bf16[48,32,256]{2,1,0:T(8,128)(2,1)S(1)}, bf16[48,32,256]{2,1,0:T(8,128)(2,1)}, u32[]{:S(2)}) copy-start(bf16[48,32,256]{2,1,0:T(8,128)(2,1)} %x_ref.1) | copy-start | bytes 2359300
  1.8 0.8 %copy-start.1 = (f32[48,256]{1,0:T(8,128)S(1)}, f32[48,256]{1,0:T(8,128)}, u32[]{:S(2)}) copy-start(f32[48,256]{1,0:T(8,128)} %constant.5.clone.sin_ref) | copy-start | bytes 147460
  2.6 0.8 %copy-start.2 = (f32[48,256]{1,0:T(8,128)S(1)}, f32[48,256]{1,0:T(8,128)}, u32[]{:S(2)}) copy-start(f32[48,256]{1,0:T(8,128)} %constant.4.clone.cos_ref) | copy-start | bytes 147460
  3.4 0.8 %copy-start.3 = (s32[32,256]{1,0:T(8,128)S(1)}, s32[32,256]{1,0:T(8,128)}, u32[]{:S(2)}) copy-start(s32[32,256]{1,0:T(8,128)} %olist_ref.1) | copy-start | bytes 98308
  4.2 0.7 %copy-start.5 = (s32[4,256]{1,0:T(4,128)S(1)}, s32[4,256]{1,0:T(4,128)}, u32[]{:S(2)}) copy-start(s32[4,256]{1,0:T(4,128)} %nb_ref.1) | copy-start | bytes 12292
  4.9 0.7 %copy-start.7 = (s32[64]{0:T(128)S(1)}, s32[64]{0:T(128)}, u32[]{:S(2)}) copy-start(s32[64]{0:T(128)} %param.14) | copy-start | bytes 772
  5.5 0.7 %copy-start.8 = (s32[64]{0:T(128)S(1)}, s32[64]{0:T(128)}, u32[]{:S(2)}) copy-start(s32[64]{0:T(128)} %param.15) | copy-start | bytes 772
  6.2 0.7 %copy-start.9 = (f32[64]{0:T(128)S(1)}, f32[64]{0:T(128)}, u32[]{:S(2)}) copy-start(f32[64]{0:T(128)} %param.16) | copy-start | bytes 772
  6.8 0.7 %copy-start.10 = (f32[64]{0:T(128)S(1)}, f32[64]{0:T(128)}, u32[]{:S(2)}) copy-start(f32[64]{0:T(128)} %param.17) | copy-start | bytes 772

commit v2 on v1

--- a/solution.py
+++ b/solution.py
@@ -65,10 +65,11 @@
 
 
 def exchange_kernel(
-    cos_ref, sin_ref, x_ref, nb_ref, opw_ref, opt_ref, oty_ref, oval_ref, ovar_ref, olist_ref, ocnt_ref,
+    angle_in, x_in, nb_in, opw_in, opt_in, oty_in, oval_in, ovar_in, olist_in, ocnt_in,
     l_ref, t_ref,
+    angle_ref, x_ref, nb_ref, opw_ref, opt_ref, oty_ref, oval_ref, ovar_ref, olist_ref, ocnt_ref,
     a1, a2, a3, send_w, send_e, recv_w, recv_e, meta, meta_l, meta_r, fore, sums, core_in, chip_sum, z_in,
-    total, total_l, total_r, relay, w8, expand, m_s, z_s, g_s, ssem, rsem,
+    total, total_l, total_r, relay, w8, expand, m_s, z_s, g_s, lsem, ssem, rsem, ready,
 ):
     tile = lax.axis_index("space")
     me = lax.axis_index("bins")
@@ -76,11 +77,25 @@
     left, right = (tile + TILES - 1) % TILES, (tile + 1) % TILES
     mate = me + 1 - 2 * core
 
+    def along(step):
+        return (tile, (me + 2 * ZC + 2 * step) % (2 * ZC))
+
     barrier = pltpu.get_barrier_semaphore()
-    partners = [(left, me), (right, me), (tile, mate)]
-    partners += [(tile, (me + 2 * k) % (2 * ZC)) for k in (4, 3, 5, 2, 6, 1, 7)]
+    partners = [(left, me), (right, me), along(1), along(-1), (tile, mate)]
     for who in partners:
         pl.semaphore_signal(barrier, inc=1, device_id=who, device_id_type=MESH)
+
+    loads = [
+        pltpu.make_async_copy(src, dst, lsem.at[n])
+        for n, (src, dst) in enumerate(
+            (
+                (x_in, x_ref), (opt_in, opt_ref), (oval_in, oval_ref), (ovar_in, ovar_ref), (nb_in, nb_ref),
+                (angle_in, angle_ref), (opw_in, opw_ref), (oty_in, oty_ref), (olist_in, olist_ref), (ocnt_in, ocnt_ref),
+            )
+        )
+    ]
+    for c in loads:
+        c.start()
 
     def copy(src, dst, n, who):
         return pltpu.make_async_remote_copy(
@@ -90,18 +105,8 @@
     lane = iota((MEM, 128), 1)
     block = lane // 32
 
-    def pack(j, _):
-        for bins, buf, half, at in ((WEST, send_w, 1, 96), (EAST, send_e, 0, 0)):
-            out = None
-            for k, (f, q) in enumerate(bins):
-                edge = x_ref[f * ND + q * SIX + j, :, 128 * half : 128 * half + 128].astype(F32)
-                edge = lanes_roll(edge, 32 * k - at)
-                out = edge if out is None else jnp.where(block == k, edge, out)
-            buf[j] = out.astype(BF16)
-        return 0
-
-    lax.fori_loop(0, SIX, pack, 0)
-
+    for c in loads[1:]:
+        c.wait()
     zeros = jnp.zeros((1, OBS), F32)
     point = opt_ref[...]
     rows = [
@@ -114,7 +119,8 @@
     freq = (jnp.where(iota((BINS, PTS), 0) >= ND, 1, 0) + 2 * me).astype(F32)
     speed = COURANT_MAX * jnp.exp(-freq * math.log(FREQ_RATIO))
     open_side = (nb_ref[...] >= 0).astype(F32)
-    cosine, sine = cos_ref[...], sin_ref[...]
+    cosine = jnp.concatenate([angle_ref[0]] * 2, axis=1)
+    sine = jnp.concatenate([angle_ref[1]] * 2, axis=1)
     cx, cy = speed * jnp.abs(cosine), speed * jnp.abs(sine)
     a1[...] = 1.0 - cx - cy
     a2[...] = cx * jnp.where(cosine > 0, open_side[0:1], open_side[1:2])
@@ -126,7 +132,22 @@
         opw_ref[...], kinds, (((0,), (0,)), ((), ())), precision=lax.Precision.HIGHEST, preferred_element_type=F32
     )
 
+    def pack(j):
+        for bins, buf, half, at in ((WEST, send_w, 1, 96), (EAST, send_e, 0, 0)):
+            out = None
+            for k, (f, q) in enumerate(bins):
+                edge = x_ref[f * ND + q * SIX + j, :, 128 * half : 128 * half + 128].astype(F32)
+                edge = lanes_roll(edge, 32 * k - at)
+                out = edge if out is None else jnp.where(block == k, edge, out)
+            buf[j] = out.astype(BF16)
+
+    loads[0].wait()
+    for j in range(SIX):
+        pack(j)
+
     pl.semaphore_wait(barrier, len(partners))
+    for step in (1, -1):
+        pl.semaphore_signal(ready.at[0], inc=1, device_id=along(step), device_id_type=MESH)
     halo = [
         copy(send_w, recv_w, 0, (right, me)),
         copy(send_e, recv_e, 1, (left, me)),
@@ -149,35 +170,43 @@
     for slot in range(MEM):
         used = jnp.where(ids[slot : slot + 1] == number, 1.0, used)
 
+    def upwind(j, f, q, inner):
+        b = f * ND + q * SIX + j
+        west = (f, q) in WEST
+        mine = int(west == inner)
+        halves = [x_ref[b, :, 128 * h : 128 * h + 128].astype(F32) for h in range(2)]
+        here_x = halves[mine]
+        if west:
+            if inner:
+                inflow = jnp.where(block == 0, lanes_roll(halves[0], 32), lanes_roll(halves[1], 32))
+            else:
+                edge = lanes_roll(recv_w[j].astype(F32), -32 * WEST.index((f, q)))
+                inflow = jnp.where(block == 0, edge, lanes_roll(halves[0], 32))
+        elif inner:
+            inflow = jnp.where(block == 3, lanes_roll(halves[1], 96), lanes_roll(halves[0], 96))
+        else:
+            edge = lanes_roll(recv_e[j].astype(F32), 96 - 32 * EAST.index((f, q)))
+            inflow = jnp.where(block == 3, edge, lanes_roll(halves[1], 96))
+        beside_y = lanes_roll(here_x, 1 if q < 2 else 127)
+        cut = slice(128 * mine, 128 * mine + 128)
+        r1, r2, r3 = a1[b : b + 1, cut], a2[b : b + 1, cut], a3[b : b + 1, cut]
+        fore[b, :, cut] = (here_x * r1 + inflow * r2 + beside_y * r3).astype(BF16)
+
+    for j in range(SIX):
+        for f in range(2):
+            for q in range(4):
+                upwind(j, f, q, True)
+
+    pl.semaphore_wait(ready.at[0], 2)
+    for step in (2, -2):
+        pl.semaphore_signal(ready.at[1], inc=1, device_id=along(step), device_id_type=MESH)
     for c in halo:
         c.wait_recv()
 
-    def propagate(j, _):
-        w_in = recv_w[j].astype(F32)
-        e_in = recv_e[j].astype(F32)
+    for j in range(SIX):
         for f in range(2):
             for q in range(4):
-                b = f * ND + q * SIX + j
-                xl = x_ref[b, :, 0:128].astype(F32)
-                xr = x_ref[b, :, 128:256].astype(F32)
-                if (f, q) in WEST:
-                    edge = lanes_roll(w_in, -32 * WEST.index((f, q)))
-                    near, far = lanes_roll(xl, 32), lanes_roll(xr, 32)
-                    ixl = jnp.where(block == 0, edge, near)
-                    ixr = jnp.where(block == 0, near, far)
-                else:
-                    edge = lanes_roll(e_in, 96 - 32 * EAST.index((f, q)))
-                    near, far = lanes_roll(xl, 96), lanes_roll(xr, 96)
-                    ixl = jnp.where(block == 3, far, near)
-                    ixr = jnp.where(block == 3, edge, far)
-                turn = 1 if q < 2 else 127
-                iyl, iyr = lanes_roll(xl, turn), lanes_roll(xr, turn)
-                r1, r2, r3 = a1[pl.ds(b, 1), :], a2[pl.ds(b, 1), :], a3[pl.ds(b, 1), :]
-                fore[b, :, 0:128] = (xl * r1[:, :128] + ixl * r2[:, :128] + iyl * r3[:, :128]).astype(BF16)
-                fore[b, :, 128:256] = (xr * r1[:, 128:] + ixr * r2[:, 128:] + iyr * r3[:, 128:]).astype(BF16)
-        return 0
-
-    lax.fori_loop(0, SIX, propagate, 0)
+                upwind(j, f, q, False)
 
     predicted = jnp.zeros((MEM, OBS), F32)
     for part in range(4):
@@ -204,12 +233,6 @@
     taper = (1.0 - distance / (2.0 * LOC_R * LOC_R)) ** 2 * used
     taper_high, taper_low = split(taper)
 
-    pair.wait_recv()
-    chip_sum[...] = sums[...] + core_in[...]
-    far = [copy(chip_sum, z_in.at[k - 1], 4 + k, (tile, (me + 2 * k) % (2 * ZC))) for k in (4, 3, 5, 2, 6, 1, 7)]
-    for c in far:
-        c.start()
-
     big_lane = iota((128, PTS), 1)
     target = 32 * ((big_lane // 32) % 4) + big_lane // 128
     source = iota((128, PTS), 0)
@@ -218,7 +241,14 @@
         expand[g] = spread
         w8[g] = dot(taper_high, spread).astype(BF16)
 
-    def turn_in(i, _):
+    pair.wait_recv()
+    pl.semaphore_wait(ready.at[1], 2)
+    chip_sum[...] = sums[...] + core_in[...]
+    far = [copy(chip_sum, z_in.at[k - 1], 4 + k, along(k)) for k in (4, 3, 5, 2, 6, 1, 7)]
+    for c in far:
+        c.start()
+
+    def turn_in(i):
         f0, f1 = fore[2 * i].astype(F32), fore[2 * i + 1].astype(F32)
         parts = []
         for q in range(4):
@@ -231,9 +261,13 @@
         turned = jnp.concatenate(parts, axis=0).T
         relay[pl.ds(2 * i, 64, stride=BINS), :] = turned[:64]
         relay[pl.ds(2 * i + 1, 64, stride=BINS), :] = turned[64:]
-        return 0
-
-    lax.fori_loop(0, BINS // 2, turn_in, 0)
+
+    for i in range(BINS // 2):
+        turn_in(i)
+
+    for g in range(GROUPS):
+        two = [relay[(2 * g + h) * BINS : (2 * g + h + 1) * BINS, :] for h in range(2)]
+        l_ref[g] = jnp.concatenate(two, axis=1).astype(BF16)
 
     for c in far:
         c.wait_recv()
@@ -245,12 +279,6 @@
     for c in beside:
         c.start()
 
-    def to_operand(g, _):
-        two = [relay[pl.ds(pl.multiple_of((2 * g + h) * BINS, 8), BINS), :] for h in range(2)]
-        l_ref[g] = jnp.concatenate(two, axis=1).astype(BF16)
-        return 0
-
-    lax.fori_loop(0, GROUPS, to_operand, 0)
     for c in beside:
         c.wait_recv()
 
@@ -339,19 +367,34 @@
 
 def per_device(x, neighbors, obs_operator, obs_point, obs_type, obs_value, obs_var, obs_list, obs_count):
     theta = 2.0 * np.pi * (np.arange(BINS) % ND + 0.5) / ND
-    cosine = jnp.asarray(np.broadcast_to(np.cos(theta)[:, None], (BINS, PTS)), F32)
-    sine = jnp.asarray(np.broadcast_to(np.sin(theta)[:, None], (BINS, PTS)), F32)
+    angles = np.stack([np.cos(theta), np.sin(theta)])[:, :, None]
+    angles = jnp.asarray(np.broadcast_to(angles, (2, BINS, 128)), F32)
     vmem = pl.BlockSpec(memory_space=pltpu.VMEM)
     tile_f32 = pltpu.VMEM((16, 128), F32)
+    operands = (
+        angles, x, neighbors, obs_operator, obs_point[None], obs_type[None], obs_value[None], obs_var[None],
+        obs_list, obs_count[None],
+    )
+    operands = [pltpu.with_memory_space_constraint(a, pltpu.HBM) for a in operands]
     operand, transform = pl.pallas_call(
         exchange_kernel,
         out_shape=(
             jax.ShapeDtypeStruct((GROUPS, BINS, PTS), BF16),
             jax.ShapeDtypeStruct((GROUPS, MEM, PTS), BF16),
         ),
-        in_specs=[vmem] * 11,
+        in_specs=[pl.BlockSpec(memory_space=pltpu.HBM)] * 10,
         out_specs=(vmem, vmem),
         scratch_shapes=[
+            pltpu.VMEM((2, BINS, 128), F32),
+            pltpu.VMEM((BINS, MEM, PTS), BF16),
+            pltpu.VMEM((4, PTS), jnp.int32),
+            pltpu.VMEM((16, BINS), F32),
+            pltpu.VMEM((1, OBS), jnp.int32),
+            pltpu.VMEM((1, OBS), jnp.int32),
+            pltpu.VMEM((1, OBS), F32),
+            pltpu.VMEM((1, OBS), F32),
+            pltpu.VMEM((MEM, PTS), jnp.int32),
+            pltpu.VMEM((1, PTS), jnp.int32),
             pltpu.VMEM((BINS, PTS), F32),
             pltpu.VMEM((BINS, PTS), F32),
             pltpu.VMEM((BINS, PTS), F32),
@@ -376,17 +419,16 @@
             pltpu.VMEM((OWN, MEM, PTS), F32),
             pltpu.VMEM((OWN, MEM, PTS), F32),
             pltpu.VMEM((OWN, MEM, PTS), F32),
+            pltpu.SemaphoreType.DMA((10,)),
             pltpu.SemaphoreType.DMA((18,)),
             pltpu.SemaphoreType.DMA((18,)),
+            pltpu.SemaphoreType.REGULAR((2,)),
         ],
         compiler_params=pltpu.CompilerParams(
             collective_id=0, has_side_effects=True, vmem_limit_bytes=40 << 20
         ),
         name="exchange",
-    )(
-        cosine, sine, x, neighbors, obs_operator, obs_point[None], obs_type[None], obs_value[None], obs_var[None],
-        obs_list, obs_count[None],
-    )
+    )(*operands)
     return pl.pallas_call(
         combine_kernel,
         out_shape=jax.ShapeDtypeStruct((BINS, MEM, PTS), BF16),

time: 48.4 us -> 40.2 us (0.83)
  local copies, waits for them, and re-layouts: 7.49 us -> 0 us
  Pallas kernels: 40.5 us -> 40 us
    unnamed x22 -> x0, local copies, waits for them, and re-layouts: 7.49 us -> none
where the time goes in v2:
time: 40.2 us; the launch traced here: 40 us
  Pallas kernels  40 us (100%)
    pallas_call x1, Pallas kernels, per_device(): pl.pallas_call(exchange_kernel, out_shape=(jax.ShapeDtypeStruct((GROUPS,...  37.4 us
    pallas_call x1, Pallas kernels, per_device(): pl.pallas_call(combine_kernel, out_shape=jax.ShapeDtypeStruct((BINS, MEM,...  2.58 us

profile of v2, /device:TPU:1, one launch (start us, length us, event | category | flops | bytes accessed | tf_op | source)
XLA Modules:
  0.0 40.0 jit_solution(17784445205175522032)
XLA Ops:
  0.0 37.4 %exchange.1 = (bf16[32,48,256]{2,1,0:T(8,128)(2,1)S(1)}, bf16[32,32,256]{2,1,0:T(8,128)(2,1)S(1)}) custom-call(f32[2,48,128]{2,1,0:T(8,128)} %constant.2.clone.angle_in, bf16[48,32,256]{2,1,0:T(8,128)(2,1)} %x_in.1, s32[4,256]{1,0:T(4,128)} %nb_in.1, f32[16,48]{1,0:T(8,128)} %opw_in.1, s32[1,64]{1,0:T(1,128)} %bitcast.6, s32[1,64]{1,0:T(1,128)} %bitcast.7, ...), custom_call_target="tpu_custom_call" | custom-call | tf_op jit(solution)/shard_map/exchange/pallas_call | solution.py:379
  37.5 2.6 %combine.1 = bf16[48,32,256]{2,1,0:T(8,128)(2,1)} custom-call(bf16[32,48,256]{2,1,0:T(8,128)(2,1)S(1)} %get-tuple-element.7.l_ref, bf16[32,32,256]{2,1,0:T(8,128)(2,1)S(1)} %get-tuple-element.8.t_ref), custom_call_target="tpu_custom_call" | custom-call | tf_op jit(solution)/shard_map/combine/pallas_call | solution.py:432

commit v3 on v2

--- a/solution.py
+++ b/solution.py
@@ -57,7 +57,7 @@
 
 
 def block_diagonal(rows, mask):
-    return jnp.concatenate([rows.astype(BF16)] * 8, axis=0) * mask
+    return jnp.concatenate([rows.astype(BF16)] * (mask.shape[0] // MEM), axis=0) * mask
 
 
 def lanes_roll(a, by):
@@ -66,10 +66,10 @@
 
 def exchange_kernel(
     angle_in, x_in, nb_in, opw_in, opt_in, oty_in, oval_in, ovar_in, olist_in, ocnt_in,
-    l_ref, t_ref,
+    mixed_ref,
     angle_ref, x_ref, nb_ref, opw_ref, opt_ref, oty_ref, oval_ref, ovar_ref, olist_ref, ocnt_ref,
-    a1, a2, a3, send_w, send_e, recv_w, recv_e, meta, meta_l, meta_r, fore, sums, core_in, chip_sum, z_in,
-    total, total_l, total_r, relay, w8, expand, m_s, z_s, g_s, lsem, ssem, rsem, ready,
+    a1, a2, a3, send_w, send_e, recv_w, recv_e, edge_w, edge_e, meta, meta_l, meta_r, fore, sums, z_in, total, total_m,
+    total_l, total_r, relay, operand, w8, expand, m_s, z_s, g_s, t_own, t_in, lsem, ssem, rsem, ready,
 ):
     tile = lax.axis_index("space")
     me = lax.axis_index("bins")
@@ -81,7 +81,7 @@
         return (tile, (me + 2 * ZC + 2 * step) % (2 * ZC))
 
     barrier = pltpu.get_barrier_semaphore()
-    partners = [(left, me), (right, me), along(1), along(-1), (tile, mate)]
+    partners = [(left, me), (right, me), (left, mate), (right, mate), (tile, mate), along(1), along(-1)]
     for who in partners:
         pl.semaphore_signal(barrier, inc=1, device_id=who, device_id_type=MESH)
 
@@ -132,6 +132,17 @@
         opw_ref[...], kinds, (((0,), (0,)), ((), ())), precision=lax.Precision.HIGHEST, preferred_element_type=F32
     )
 
+    at_obs = dot(jnp.concatenate([open_side, jnp.zeros((4, PTS), F32)], axis=0).astype(BF16), here)
+    obs_col, obs_row = point // ROWS - tile * (PTS // ROWS), point % ROWS
+    first_col = jnp.where(obs_col == 0, at_obs[0:1], 0.0)
+    last_col = jnp.where(obs_col == PTS // ROWS - 1, at_obs[1:2], 0.0)
+    in_row = (iota((ROWS, OBS), 0) == obs_row).astype(F32)
+    carried = weights * cx[:, :OBS]
+    for j in range(SIX):
+        for bins, buf, on in ((WEST, edge_w, first_col), (EAST, edge_e, last_col)):
+            rows4 = [in_row * (carried[f * ND + q * SIX + j : f * ND + q * SIX + j + 1] * on) for f, q in bins]
+            buf[j] = jnp.concatenate(rows4, axis=0).astype(BF16)
+
     def pack(j):
         for bins, buf, half, at in ((WEST, send_w, 1, 96), (EAST, send_e, 0, 0)):
             out = None
@@ -157,6 +168,49 @@
     for c in halo:
         c.start()
 
+    def upwind(j, f, q, part):
+        b = f * ND + q * SIX + j
+        west = (f, q) in WEST
+        mine = int(west == (part == 0))
+        halves = [x_ref[b, :, 128 * h : 128 * h + 128].astype(F32) for h in range(2)]
+        here_x = halves[mine]
+        if part == 2:
+            spot = (WEST if west else EAST).index((f, q))
+            edge = (recv_w if west else recv_e)[j].astype(F32)
+            edge = lanes_roll(edge, (0 if west else 96) - 32 * spot)
+        else:
+            edge = jnp.zeros((MEM, 128), F32)
+        if west:
+            other = lanes_roll(halves[0], 32) if part == 0 else edge
+            inflow = jnp.where(block == 0, other, lanes_roll(here_x, 32))
+        else:
+            other = lanes_roll(halves[1], 96) if part == 0 else edge
+            inflow = jnp.where(block == 3, other, lanes_roll(here_x, 96))
+        beside_y = lanes_roll(here_x, 1 if q < 2 else 127)
+        cut = slice(128 * mine, 128 * mine + 128)
+        r1, r2, r3 = a1[b : b + 1, cut], a2[b : b + 1, cut], a3[b : b + 1, cut]
+        fore[b, :, cut] = (here_x * r1 + inflow * r2 + beside_y * r3).astype(BF16)
+
+    def upwind_all(*parts):
+        for j in range(SIX):
+            for f in range(2):
+                for q in range(4):
+                    for part in parts:
+                        upwind(j, f, q, part)
+
+    upwind_all(0, 1)
+
+    predicted = jnp.zeros((MEM, OBS), F32)
+    for part in range(4):
+        at = dot(fore[12 * part : 12 * part + 12].reshape(12 * MEM, PTS), here)
+        for i in range(12):
+            b = 12 * part + i
+            predicted += at[MEM * i : MEM * (i + 1)] * weights[b : b + 1]
+
+    pl.semaphore_wait(ready.at[0], 2)
+    for step in (2, -2):
+        pl.semaphore_signal(ready.at[1], inc=1, device_id=along(step), device_id_type=MESH)
+
     ids = jnp.where(iota((MEM, PTS), 0) < ocnt_ref[...], olist_ref[...] - (tile - 1) * OBS, -1)
     ids = jnp.where(olist_ref[...] >= 0, ids, -1)
     low, high = ids[:, :128], ids[:, 128:]
@@ -170,53 +224,17 @@
     for slot in range(MEM):
         used = jnp.where(ids[slot : slot + 1] == number, 1.0, used)
 
-    def upwind(j, f, q, inner):
-        b = f * ND + q * SIX + j
-        west = (f, q) in WEST
-        mine = int(west == inner)
-        halves = [x_ref[b, :, 128 * h : 128 * h + 128].astype(F32) for h in range(2)]
-        here_x = halves[mine]
-        if west:
-            if inner:
-                inflow = jnp.where(block == 0, lanes_roll(halves[0], 32), lanes_roll(halves[1], 32))
-            else:
-                edge = lanes_roll(recv_w[j].astype(F32), -32 * WEST.index((f, q)))
-                inflow = jnp.where(block == 0, edge, lanes_roll(halves[0], 32))
-        elif inner:
-            inflow = jnp.where(block == 3, lanes_roll(halves[1], 96), lanes_roll(halves[0], 96))
-        else:
-            edge = lanes_roll(recv_e[j].astype(F32), 96 - 32 * EAST.index((f, q)))
-            inflow = jnp.where(block == 3, edge, lanes_roll(halves[1], 96))
-        beside_y = lanes_roll(here_x, 1 if q < 2 else 127)
-        cut = slice(128 * mine, 128 * mine + 128)
-        r1, r2, r3 = a1[b : b + 1, cut], a2[b : b + 1, cut], a3[b : b + 1, cut]
-        fore[b, :, cut] = (here_x * r1 + inflow * r2 + beside_y * r3).astype(BF16)
-
+    halo[0].wait_recv()
+    halo[1].wait_recv()
     for j in range(SIX):
-        for f in range(2):
-            for q in range(4):
-                upwind(j, f, q, True)
-
-    pl.semaphore_wait(ready.at[0], 2)
-    for step in (2, -2):
-        pl.semaphore_signal(ready.at[1], inc=1, device_id=along(step), device_id_type=MESH)
-    for c in halo:
-        c.wait_recv()
-
-    for j in range(SIX):
-        for f in range(2):
-            for q in range(4):
-                upwind(j, f, q, False)
-
-    predicted = jnp.zeros((MEM, OBS), F32)
-    for part in range(4):
-        at = dot(fore[12 * part : 12 * part + 12].reshape(12 * MEM, PTS), here)
-        for i in range(12):
-            b = 12 * part + i
-            predicted += at[MEM * i : MEM * (i + 1)] * weights[b : b + 1]
+        predicted += dot(recv_w[j], edge_w[j]) + dot(recv_e[j], edge_e[j])
     sums[...] = jnp.concatenate([predicted[:16], predicted[16:]], axis=1)
-    pair = copy(sums, core_in, 4, (tile, mate))
-    pair.start()
+    pl.semaphore_wait(ready.at[1], 2)
+    far = [copy(sums, z_in.at[k - 1], 4 + k, along(k)) for k in (1, 7, 2, 6, 3, 5, 4)]
+    for c in far:
+        c.start()
+    halo[2].wait_recv()
+    halo[3].wait_recv()
 
     metas = jnp.concatenate(
         [
@@ -241,12 +259,7 @@
         expand[g] = spread
         w8[g] = dot(taper_high, spread).astype(BF16)
 
-    pair.wait_recv()
-    pl.semaphore_wait(ready.at[1], 2)
-    chip_sum[...] = sums[...] + core_in[...]
-    far = [copy(chip_sum, z_in.at[k - 1], 4 + k, along(k)) for k in (4, 3, 5, 2, 6, 1, 7)]
-    for c in far:
-        c.start()
+    upwind_all(2)
 
     def turn_in(i):
         f0, f1 = fore[2 * i].astype(F32), fore[2 * i + 1].astype(F32)
@@ -265,25 +278,29 @@
     for i in range(BINS // 2):
         turn_in(i)
 
-    for g in range(GROUPS):
-        two = [relay[(2 * g + h) * BINS : (2 * g + h + 1) * BINS, :] for h in range(2)]
-        l_ref[g] = jnp.concatenate(two, axis=1).astype(BF16)
+    for t in range(2 * GROUPS):
+        operand[t] = relay[t * BINS : (t + 1) * BINS, :].astype(BF16)
 
     for c in far:
         c.wait_recv()
-    acc = chip_sum[...]
+    acc = sums[...]
     for k in range(7):
         acc += z_in[k]
     total[...] = acc
-    beside = [copy(total, total_l, 12, (right, me)), copy(total, total_r, 13, (left, me))]
+    beside = [
+        copy(total, total_l.at[0], 12, (right, me)),
+        copy(total, total_r.at[0], 13, (left, me)),
+        copy(total, total_l.at[1], 14, (right, mate)),
+        copy(total, total_r.at[1], 15, (left, mate)),
+        copy(total, total_m, 16, (tile, mate)),
+    ]
     for c in beside:
         c.start()
-
     for c in beside:
         c.wait_recv()
 
     half = iota((16, 128), 1) < OBS
-    pl_, po, pr = total_l[...], total[...], total_r[...]
+    pl_, po, pr = total_l[0] + total_l[1], total[...] + total_m[...], total_r[0] + total_r[1]
     first = jnp.where(half, pl_, lanes_roll(po, 64)), jnp.where(half, pr, 0.0)
     second = jnp.where(half, lanes_roll(pl_, 64), po), jnp.where(half, lanes_roll(pr, 64), 0.0)
     seen = jnp.concatenate([jnp.concatenate(first, axis=1), jnp.concatenate(second, axis=1)], axis=0)
@@ -309,24 +326,29 @@
     inv_scale = lax.rsqrt(norm)
     root_scale = jnp.sqrt(inv_scale)
 
+    same_half = same[:128, :128]
     for it in range(NS_ITERS):
         for g in range(OWN):
-            current = m_s[g] * inv_scale[g : g + 1] if it == 0 else m_s[g]
-            step = 0.5 * (eye - current)
-            operand = block_diagonal(step, same)
-            if it == 0:
-                moved = current + dot(current.astype(BF16), operand)
-                z_s[g] = eye + step
-            elif it == NS_ITERS - 1:
-                inverse = z_s[g]
-                z_s[g] = inverse + dot(inverse.astype(BF16), operand)
-                continue
-            else:
-                inverse = z_s[g]
-                both = dot(jnp.concatenate([current, inverse], axis=0).astype(BF16), operand)
-                moved = current + both[:MEM]
-                z_s[g] = inverse + both[MEM:]
-            m_s[g] = moved + dot(moved.astype(BF16), operand)
+            for h in range(2):
+                cut = slice(128 * h, 128 * h + 128)
+                current = m_s[g, :, cut]
+                if it == 0:
+                    current = current * inv_scale[g : g + 1, cut]
+                step = 0.5 * (eye[:, cut] - current)
+                weight = block_diagonal(step, same_half)
+                if it == 0:
+                    moved = current + dot(current.astype(BF16), weight)
+                    z_s[g, :, cut] = eye[:, cut] + step
+                elif it == NS_ITERS - 1:
+                    inverse = z_s[g, :, cut]
+                    z_s[g, :, cut] = inverse + dot(inverse.astype(BF16), weight)
+                    continue
+                else:
+                    inverse = z_s[g, :, cut]
+                    both = dot(jnp.concatenate([current, inverse], axis=0).astype(BF16), weight)
+                    moved = current + both[:MEM]
+                    z_s[g, :, cut] = inverse + both[MEM:]
+                m_s[g, :, cut] = moved + dot(moved.astype(BF16), weight)
 
     swaps = []
     for g in range(OWN):
@@ -335,27 +357,34 @@
         shift = folded(dot(stacked(root * half_step), same))
         mix = root + shift
         mix = mix + (1.0 - jnp.sum(mix, axis=0, keepdims=True)) * (1.0 / MEM)
-        t_ref[core * OWN + g] = mix.astype(BF16)
+        t_own[g] = mix.astype(BF16)
         if g % 4 == 3:
-            part = t_ref.at[pl.ds(core * OWN + g - 3, 4)]
-            swap = copy(part, part, 14 + g // 4, (tile, mate))
+            part = pl.ds(g - 3, 4)
+            swap = copy(t_own.at[part], t_in.at[part], 17 + g // 4, (tile, mate))
             swap.start()
             swaps.append(swap)
-    for c in swaps:
-        c.wait()
-    for c in halo + [pair] + far + beside:
+
+    def apply(owner, g, transform):
+        for h in range(2):
+            t = 2 * OWN * owner + 2 * g + h
+            weight = block_diagonal(transform[g, :, 128 * h : 128 * h + 128], same_half)
+            mixed_ref[pl.ds(pl.multiple_of(t * BINS, 8), BINS), :] = dot(operand[t], weight)
+
+    for g in range(OWN):
+        apply(core, g, t_own)
+    for n, c in enumerate(swaps):
+        c.wait_recv()
+        for g in range(4 * n, 4 * n + 4):
+            apply(1 - core, g, t_in)
+    for c in halo + far + beside + swaps:
         c.wait_send()
 
 
-def combine_kernel(l_ref, t_ref, out_ref, relay):
-    same = (iota((PTS, PTS), 0) // MEM == iota((PTS, PTS), 1) // MEM).astype(BF16)
-    for g in range(GROUPS):
-        mixed = dot(l_ref[g], block_diagonal(t_ref[g], same))
-        for h in range(2):
-            relay[(2 * g + h) * BINS : (2 * g + h + 1) * BINS, :] = mixed[:, 128 * h : 128 * h + 128]
+def place_kernel(mixed_ref, out_hbm, out_ref, sem):
     lane = iota((MEM, 128), 1)
+    copies = []
     for i in range(BINS // 2):
-        two = [relay[pl.ds(2 * i + k, 64, stride=BINS), :] for k in range(2)]
+        two = [mixed_ref[pl.ds(2 * i + k, 64, stride=BINS), :] for k in range(2)]
         turned = jnp.concatenate(two, axis=0).T
         q = [turned[MEM * k : MEM * (k + 1)] for k in range(4)]
         for h in range(2):
@@ -363,6 +392,13 @@
             cut = slice(128 * h, 128 * h + 128)
             out_ref[2 * i, :, cut] = jnp.where(lane < 64, a, lanes_roll(b, 64)).astype(BF16)
             out_ref[2 * i + 1, :, cut] = jnp.where(lane < 64, lanes_roll(a, 64), b).astype(BF16)
+        if i % 4 == 3:
+            part = pl.ds(2 * i - 6, 8)
+            c = pltpu.make_async_copy(out_ref.at[part], out_hbm.at[part], sem.at[i // 4])
+            c.start()
+            copies.append(c)
+    for c in copies:
+        c.wait()
 
 
 def per_device(x, neighbors, obs_operator, obs_point, obs_type, obs_value, obs_var, obs_list, obs_count):
@@ -376,14 +412,11 @@
         obs_list, obs_count[None],
     )
     operands = [pltpu.with_memory_space_constraint(a, pltpu.HBM) for a in operands]
-    operand, transform = pl.pallas_call(
+    mixed = pl.pallas_call(
         exchange_kernel,
-        out_shape=(
-            jax.ShapeDtypeStruct((GROUPS, BINS, PTS), BF16),
-            jax.ShapeDtypeStruct((GROUPS, MEM, PTS), BF16),
-        ),
+        out_shape=jax.ShapeDtypeStruct((2 * GROUPS * BINS, 128), F32),
         in_specs=[pl.BlockSpec(memory_space=pltpu.HBM)] * 10,
-        out_specs=(vmem, vmem),
+        out_specs=vmem,
         scratch_shapes=[
             pltpu.VMEM((2, BINS, 128), F32),
             pltpu.VMEM((BINS, MEM, PTS), BF16),
@@ -402,26 +435,30 @@
             pltpu.VMEM((SIX, MEM, 128), BF16),
             pltpu.VMEM((SIX, MEM, 128), BF16),
             pltpu.VMEM((SIX, MEM, 128), BF16),
+            pltpu.VMEM((SIX, 128, OBS), BF16),
+            pltpu.VMEM((SIX, 128, OBS), BF16),
             pltpu.VMEM((8, 128), F32),
             pltpu.VMEM((8, 128), F32),
             pltpu.VMEM((8, 128), F32),
             pltpu.VMEM((BINS, MEM, PTS), BF16),
             tile_f32,
-            tile_f32,
-            tile_f32,
             pltpu.VMEM((7, 16, 128), F32),
             tile_f32,
             tile_f32,
-            tile_f32,
+            pltpu.VMEM((2, 16, 128), F32),
+            pltpu.VMEM((2, 16, 128), F32),
             pltpu.VMEM((64 * BINS, 128), F32),
+            pltpu.VMEM((2 * GROUPS, BINS, 128), BF16),
             pltpu.VMEM((OWN, NEAR, PTS), BF16),
             pltpu.VMEM((OWN, 128, PTS), BF16),
             pltpu.VMEM((OWN, MEM, PTS), F32),
             pltpu.VMEM((OWN, MEM, PTS), F32),
             pltpu.VMEM((OWN, MEM, PTS), F32),
+            pltpu.VMEM((OWN, MEM, PTS), BF16),
+            pltpu.VMEM((OWN, MEM, PTS), BF16),
             pltpu.SemaphoreType.DMA((10,)),
-            pltpu.SemaphoreType.DMA((18,)),
-            pltpu.SemaphoreType.DMA((18,)),
+            pltpu.SemaphoreType.DMA((21,)),
+            pltpu.SemaphoreType.DMA((21,)),
             pltpu.SemaphoreType.REGULAR((2,)),
         ],
         compiler_params=pltpu.CompilerParams(
@@ -430,14 +467,14 @@
         name="exchange",
     )(*operands)
     return pl.pallas_call(
-        combine_kernel,
+        place_kernel,
         out_shape=jax.ShapeDtypeStruct((BINS, MEM, PTS), BF16),
-        in_specs=[vmem, vmem],
-        out_specs=vmem,
-        scratch_shapes=[pltpu.VMEM((64 * BINS, 128), F32)],
+        in_specs=[vmem],
+        out_specs=pl.BlockSpec(memory_space=pl.ANY),
+        scratch_shapes=[pltpu.VMEM((BINS, MEM, PTS), BF16), pltpu.SemaphoreType.DMA((SIX,))],
         compiler_params=pltpu.CompilerParams(vmem_limit_bytes=40 << 20),
-        name="combine",
-    )(operand, transform)
+        name="place",
+    )(mixed)
 
 
 def solution(mesh):

time: 40.2 us -> 37.6 us (0.935)
  Pallas kernels: 40 us -> 37.5 us
    pallas_call x2, Pallas kernels: 40 us -> 37.5 us  [the longest x1 36.1 us: per_device(): pl.pallas_call(exchange_kernel, out_shape=jax.ShapeDtypeStruct((2 * GROUP...]
where the time goes in v3:
time: 37.6 us; the launch traced here: 37.5 us
  Pallas kernels  37.5 us (100%)
    pallas_call x1, Pallas kernels, per_device(): pl.pallas_call(exchange_kernel, out_shape=jax.ShapeDtypeStruct((2 * GROUP...  36.1 us
    pallas_call x1, Pallas kernels, per_device(): pl.pallas_call(place_kernel, out_shape=jax.ShapeDtypeStruct((BINS, MEM, P...  1.41 us

profile of v3, /device:TPU:1, one launch (start us, length us, event | category | flops | bytes accessed | tf_op | source)
XLA Modules:
  0.0 37.5 jit_solution(17818329975548144147)
XLA Ops:
  0.0 36.1 %exchange.1.mixed_ref = f32[3072,128]{1,0:T(8,128)S(1)} custom-call(f32[2,48,128]{2,1,0:T(8,128)} %constant.2.clone.angle_in, bf16[48,32,256]{2,1,0:T(8,128)(2,1)} %x_in.1, s32[4,256]{1,0:T(4,128)} %nb_in.1, f32[16,48]{1,0:T(8,128)} %opw_in.1, s32[1,64]{1,0:T(1,128)} %bitcast.6, s32[1,64]{1,0:T(1,128)} %bitcast.7, f32[1,64]{1,0:T(1,128)} %bitcast.8, ...), custom_call_target="tpu_custom_call" | custom-call | tf_op jit(solution)/shard_map/exchange/pallas_call | solution.py:415
  36.1 1.4 %place.1 = bf16[48,32,256]{2,1,0:T(8,128)(2,1)} custom-call(f32[3072,128]{1,0:T(8,128)S(1)} %exchange.1.mixed_ref), custom_call_target="tpu_custom_call" | custom-call | tf_op jit(solution)/shard_map/place/pallas_call | solution.py:469

commit v4 on v3

--- a/solution.py
+++ b/solution.py
@@ -25,6 +25,8 @@
 GROUPS = 2 * OWN
 TILES = 32
 ZC = 8
+BATCHES = (range(8), range(8, 16))
+SENT = (0, 8, 12, 16)
 SIX = 6
 WEST = ((0, 0), (0, 3), (1, 0), (1, 3))
 EAST = ((0, 1), (0, 2), (1, 1), (1, 2))
@@ -157,16 +159,18 @@
         pack(j)
 
     pl.semaphore_wait(barrier, len(partners))
-    for step in (1, -1):
-        pl.semaphore_signal(ready.at[0], inc=1, device_id=along(step), device_id_type=MESH)
     halo = [
         copy(send_w, recv_w, 0, (right, me)),
         copy(send_e, recv_e, 1, (left, me)),
         copy(meta, meta_l, 2, (right, me)),
         copy(meta, meta_r, 3, (left, me)),
     ]
-    for c in halo:
-        c.start()
+    halo[0].start()
+    halo[1].start()
+    for step in (1, -1):
+        pl.semaphore_signal(ready.at[0], inc=1, device_id=along(step), device_id_type=MESH)
+    halo[2].start()
+    halo[3].start()
 
     def upwind(j, f, q, part):
         b = f * ND + q * SIX + j
@@ -230,7 +234,11 @@
         predicted += dot(recv_w[j], edge_w[j]) + dot(recv_e[j], edge_e[j])
     sums[...] = jnp.concatenate([predicted[:16], predicted[16:]], axis=1)
     pl.semaphore_wait(ready.at[1], 2)
-    far = [copy(sums, z_in.at[k - 1], 4 + k, along(k)) for k in (1, 7, 2, 6, 3, 5, 4)]
+    chip = me // 2
+    far = []
+    for n in range(ZC - 1):
+        away = (n + (n + ZC - chip) // ZC + ZC - chip) % ZC
+        far.append(copy(sums, z_in.at[away - 1], 4 + away, along(away)))
     for c in far:
         c.start()
     halo[2].wait_recv()
@@ -327,54 +335,62 @@
     root_scale = jnp.sqrt(inv_scale)
 
     same_half = same[:128, :128]
-    for it in range(NS_ITERS):
-        for g in range(OWN):
-            for h in range(2):
-                cut = slice(128 * h, 128 * h + 128)
-                current = m_s[g, :, cut]
-                if it == 0:
-                    current = current * inv_scale[g : g + 1, cut]
-                step = 0.5 * (eye[:, cut] - current)
-                weight = block_diagonal(step, same_half)
-                if it == 0:
-                    moved = current + dot(current.astype(BF16), weight)
-                    z_s[g, :, cut] = eye[:, cut] + step
-                elif it == NS_ITERS - 1:
-                    inverse = z_s[g, :, cut]
-                    z_s[g, :, cut] = inverse + dot(inverse.astype(BF16), weight)
-                    continue
-                else:
-                    inverse = z_s[g, :, cut]
-                    both = dot(jnp.concatenate([current, inverse], axis=0).astype(BF16), weight)
-                    moved = current + both[:MEM]
-                    z_s[g, :, cut] = inverse + both[MEM:]
-                m_s[g, :, cut] = moved + dot(moved.astype(BF16), weight)
-
-    swaps = []
-    for g in range(OWN):
+
+    def newton(groups):
+        for it in range(NS_ITERS):
+            for g in groups:
+                for h in range(2):
+                    cut = slice(128 * h, 128 * h + 128)
+                    current = m_s[g, :, cut]
+                    if it == 0:
+                        current = current * inv_scale[g : g + 1, cut]
+                    step = 0.5 * (eye[:, cut] - current)
+                    weight = block_diagonal(step, same_half)
+                    if it == 0:
+                        moved = current + dot(current.astype(BF16), weight)
+                        z_s[g, :, cut] = eye[:, cut] + step
+                    elif it == NS_ITERS - 1:
+                        inverse = z_s[g, :, cut]
+                        z_s[g, :, cut] = inverse + dot(inverse.astype(BF16), weight)
+                        continue
+                    else:
+                        inverse = z_s[g, :, cut]
+                        both = dot(jnp.concatenate([current, inverse], axis=0).astype(BF16), weight)
+                        moved = current + both[:MEM]
+                        z_s[g, :, cut] = inverse + both[MEM:]
+                    m_s[g, :, cut] = moved + dot(moved.astype(BF16), weight)
+
+    def mix(g):
         root = z_s[g] * root_scale[g : g + 1]
         half_step = jnp.sum(root * g_s[g], axis=0, keepdims=True)
         shift = folded(dot(stacked(root * half_step), same))
-        mix = root + shift
-        mix = mix + (1.0 - jnp.sum(mix, axis=0, keepdims=True)) * (1.0 / MEM)
-        t_own[g] = mix.astype(BF16)
-        if g % 4 == 3:
-            part = pl.ds(g - 3, 4)
-            swap = copy(t_own.at[part], t_in.at[part], 17 + g // 4, (tile, mate))
-            swap.start()
-            swaps.append(swap)
+        mixed = root + shift
+        mixed = mixed + (1.0 - jnp.sum(mixed, axis=0, keepdims=True)) * (1.0 / MEM)
+        t_own[g] = mixed.astype(BF16)
+
+    swaps = []
+    for groups in BATCHES:
+        newton(groups)
+        for g in groups:
+            mix(g)
+            if g + 1 in SENT:
+                first = SENT[SENT.index(g + 1) - 1]
+                part = pl.ds(first, g + 1 - first)
+                swap = copy(t_own.at[part], t_in.at[part], 17 + len(swaps), (tile, mate))
+                swap.start()
+                swaps.append(swap)
 
     def apply(owner, g, transform):
         for h in range(2):
             t = 2 * OWN * owner + 2 * g + h
             weight = block_diagonal(transform[g, :, 128 * h : 128 * h + 128], same_half)
-            mixed_ref[pl.ds(pl.multiple_of(t * BINS, 8), BINS), :] = dot(operand[t], weight)
+            mixed_ref[pl.ds(t, BINS, stride=2 * GROUPS), :] = dot(operand[t], weight)
 
     for g in range(OWN):
         apply(core, g, t_own)
     for n, c in enumerate(swaps):
         c.wait_recv()
-        for g in range(4 * n, 4 * n + 4):
+        for g in range(SENT[n], SENT[n + 1]):
             apply(1 - core, g, t_in)
     for c in halo + far + beside + swaps:
         c.wait_send()
@@ -384,8 +400,7 @@
     lane = iota((MEM, 128), 1)
     copies = []
     for i in range(BINS // 2):
-        two = [mixed_ref[pl.ds(2 * i + k, 64, stride=BINS), :] for k in range(2)]
-        turned = jnp.concatenate(two, axis=0).T
+        turned = mixed_ref[128 * i : 128 * i + 128, :].T
         q = [turned[MEM * k : MEM * (k + 1)] for k in range(4)]
         for h in range(2):
             a, b = q[2 * h], q[2 * h + 1]
@@ -457,8 +472,8 @@
             pltpu.VMEM((OWN, MEM, PTS), BF16),
             pltpu.VMEM((OWN, MEM, PTS), BF16),
             pltpu.SemaphoreType.DMA((10,)),
-            pltpu.SemaphoreType.DMA((21,)),
-            pltpu.SemaphoreType.DMA((21,)),
+            pltpu.SemaphoreType.DMA((20,)),
+            pltpu.SemaphoreType.DMA((20,)),
             pltpu.SemaphoreType.REGULAR((2,)),
         ],
         compiler_params=pltpu.CompilerParams(

time: 37.6 us -> 37.5 us (level)
  no operation moved by 1% of the time
where the time goes in v4:
time: 37.5 us; the launch traced here: 37.3 us
  Pallas kernels  37.3 us (99%)
    pallas_call x1, Pallas kernels, per_device(): pl.pallas_call(exchange_kernel, out_shape=jax.ShapeDtypeStruct((2 * GROUP...  36 us
    pallas_call x1, Pallas kernels, per_device(): pl.pallas_call(place_kernel, out_shape=jax.ShapeDtypeStruct((BINS, MEM, P...  1.33 us

profile of v4, /device:TPU:1, one launch (start us, length us, event | category | flops | bytes accessed | tf_op | source)
XLA Modules:
  0.0 37.3 jit_solution(4260806333029057089)
XLA Ops:
  0.0 36.0 %exchange.1.mixed_ref = f32[3072,128]{1,0:T(8,128)S(1)} custom-call(f32[2,48,128]{2,1,0:T(8,128)} %constant.2.clone.angle_in, bf16[48,32,256]{2,1,0:T(8,128)(2,1)} %x_in.1, s32[4,256]{1,0:T(4,128)} %nb_in.1, f32[16,48]{1,0:T(8,128)} %opw_in.1, s32[1,64]{1,0:T(1,128)} %bitcast.6, s32[1,64]{1,0:T(1,128)} %bitcast.7, f32[1,64]{1,0:T(1,128)} %bitcast.8, ...), custom_call_target="tpu_custom_call" | custom-call | tf_op jit(solution)/shard_map/exchange/pallas_call | solution.py:430
  36.0 1.3 %place.1 = bf16[48,32,256]{2,1,0:T(8,128)(2,1)} custom-call(f32[3072,128]{1,0:T(8,128)S(1)} %exchange.1.mixed_ref), custom_call_target="tpu_custom_call" | custom-call | tf_op jit(solution)/shard_map/place/pallas_call | solution.py:484

commit v5 on v4

--- a/solution.py
+++ b/solution.py
@@ -143,7 +143,7 @@
     for j in range(SIX):
         for bins, buf, on in ((WEST, edge_w, first_col), (EAST, edge_e, last_col)):
             rows4 = [in_row * (carried[f * ND + q * SIX + j : f * ND + q * SIX + j + 1] * on) for f, q in bins]
-            buf[j] = jnp.concatenate(rows4, axis=0).astype(BF16)
+            buf[128 * j : 128 * j + 128, :] = jnp.concatenate(rows4, axis=0).astype(BF16)
 
     def pack(j):
         for bins, buf, half, at in ((WEST, send_w, 1, 96), (EAST, send_e, 0, 0)):
@@ -230,8 +230,8 @@
 
     halo[0].wait_recv()
     halo[1].wait_recv()
-    for j in range(SIX):
-        predicted += dot(recv_w[j], edge_w[j]) + dot(recv_e[j], edge_e[j])
+    for buf, weight in ((recv_w, edge_w), (recv_e, edge_e)):
+        predicted += dot(jnp.concatenate([buf[j] for j in range(SIX)], axis=1), weight[...])
     sums[...] = jnp.concatenate([predicted[:16], predicted[16:]], axis=1)
     pl.semaphore_wait(ready.at[1], 2)
     chip = me // 2
@@ -324,15 +324,19 @@
 
     eye = (iota((MEM, PTS), 0) == iota((MEM, PTS), 1) % MEM).astype(F32)
     same = (iota((PTS, PTS), 0) // MEM == iota((PTS, PTS), 1) // MEM).astype(BF16)
-    squares = []
+    inv_scale, root_scale = {}, {}
+    for groups in BATCHES:
+        squares = []
+        for g in groups:
+            matrix = eye + dot(y, w8[g] * y_t) * (1.0 / (MEM - 1))
+            m_s[g] = matrix
+            squares.append(jnp.sum(matrix * matrix, axis=0, keepdims=True))
+        norm = folded(dot(stacked(jnp.concatenate(squares, axis=0)), same))
+        for n, g in enumerate(groups):
+            inv_scale[g] = lax.rsqrt(norm[n : n + 1])
+            root_scale[g] = jnp.sqrt(inv_scale[g])
     for g in range(OWN):
-        matrix = eye + dot(y, w8[g] * y_t) * (1.0 / (MEM - 1))
-        m_s[g] = matrix
-        squares.append(jnp.sum(matrix * matrix, axis=0, keepdims=True))
         g_s[g] = folded(dot(pulls, expand[g]))
-    norm = folded(dot(stacked(jnp.concatenate(squares, axis=0)), same))
-    inv_scale = lax.rsqrt(norm)
-    root_scale = jnp.sqrt(inv_scale)
 
     same_half = same[:128, :128]
 
@@ -343,7 +347,7 @@
                     cut = slice(128 * h, 128 * h + 128)
                     current = m_s[g, :, cut]
                     if it == 0:
-                        current = current * inv_scale[g : g + 1, cut]
+                        current = current * inv_scale[g][:, cut]
                     step = 0.5 * (eye[:, cut] - current)
                     weight = block_diagonal(step, same_half)
                     if it == 0:
@@ -361,7 +365,7 @@
                     m_s[g, :, cut] = moved + dot(moved.astype(BF16), weight)
 
     def mix(g):
-        root = z_s[g] * root_scale[g : g + 1]
+        root = z_s[g] * root_scale[g]
         half_step = jnp.sum(root * g_s[g], axis=0, keepdims=True)
         shift = folded(dot(stacked(root * half_step), same))
         mixed = root + shift
@@ -450,8 +454,8 @@
             pltpu.VMEM((SIX, MEM, 128), BF16),
             pltpu.VMEM((SIX, MEM, 128), BF16),
             pltpu.VMEM((SIX, MEM, 128), BF16),
-            pltpu.VMEM((SIX, 128, OBS), BF16),
-            pltpu.VMEM((SIX, 128, OBS), BF16),
+            pltpu.VMEM((SIX * 128, OBS), BF16),
+            pltpu.VMEM((SIX * 128, OBS), BF16),
             pltpu.VMEM((8, 128), F32),
             pltpu.VMEM((8, 128), F32),
             pltpu.VMEM((8, 128), F32),

time: 37.5 us -> 37.3 us (level)
  no operation moved by 1% of the time
where the time goes in v5:
time: 37.3 us; the launch traced here: 37.2 us
  Pallas kernels  37.1 us (99%)
    pallas_call x1, Pallas kernels, per_device(): pl.pallas_call(exchange_kernel, out_shape=jax.ShapeDtypeStruct((2 * GROUP...  35.8 us
    pallas_call x1, Pallas kernels, per_device(): pl.pallas_call(place_kernel, out_shape=jax.ShapeDtypeStruct((BINS, MEM, P...  1.33 us

profile of v5, /device:TPU:1, one launch (start us, length us, event | category | flops | bytes accessed | tf_op | source)
XLA Modules:
  0.0 37.2 jit_solution(17860792105795562514)
XLA Ops:
  0.0 35.8 %exchange.1.mixed_ref = f32[3072,128]{1,0:T(8,128)S(1)} custom-call(f32[2,48,128]{2,1,0:T(8,128)} %constant.2.clone.angle_in, bf16[48,32,256]{2,1,0:T(8,128)(2,1)} %x_in.1, s32[4,256]{1,0:T(4,128)} %nb_in.1, f32[16,48]{1,0:T(8,128)} %opw_in.1, s32[1,64]{1,0:T(1,128)} %bitcast.6, s32[1,64]{1,0:T(1,128)} %bitcast.7, f32[1,64]{1,0:T(1,128)} %bitcast.8, ...), custom_call_target="tpu_custom_call" | custom-call | tf_op jit(solution)/shard_map/exchange/pallas_call | solution.py:434
  35.8 1.3 %place.1 = bf16[48,32,256]{2,1,0:T(8,128)(2,1)} custom-call(f32[3072,128]{1,0:T(8,128)S(1)} %exchange.1.mixed_ref), custom_call_target="tpu_custom_call" | custom-call | tf_op jit(solution)/shard_map/place/pallas_call | solution.py:488
